TPU v7x, 32 devices: a whole 2x2x4 slice. The times are simulated.
32 devices in a mesh: ev: 4 (over z), site: 8 (over y, x, core).
Axes of the slice: x: 2, y: 2, z: 4, core: 2. Of those that a mesh axis runs over, the one named last changes fastest.
Arguments:
- ruptures: float32 [6, 64], P(None, ('ev', 'site')), may hold values from -60 to 260, as said below
- event_rupture: int32 [32], P(('ev', 'site')), may hold values from 0 to 63
- epsilon: bfloat16 [2, 32, 4096], P(None, ('ev', 'site')), may hold values from -4 to 4
- site_coords: float32 [2, 4096], replicated, may hold values from 0 to 200
- vulnerability: bfloat16 [128, 40], replicated, may hold values from 0 to 1
- taxo_measure: int32 [128], replicated, may hold values from 0 to 1
- taxo_offset: int32 [128], replicated, may hold values from 0 to 24
- asset_site: int32 [81920], P('site'), may hold values from 0 to 511
- asset_taxo: int32 [81920], P('site'), may hold values from 0 to 127
- asset_tract: int32 [81920], P('site'), may hold values from 0 to 7
- asset_value: float32 [81920], P('site'), may hold values from 0.002 to 0.05
Outputs:
- losses: float32 [8, 32, 128], P('site', 'ev')
Inputs may be any that keep to these rules, and one draw needn't show every extreme that they name: Asset a stands at site (a // 10240) * 512 + asset_site[a]. `ruptures`: every rupture is 5 km long or more, its depth 2 to 20 km and its magnitude 5 to 8.
All inputs are finite; a program needn't handle non-finite values.
Results may differ from a plain program's by a relative error of at most 0.00064.
Values may be sent and summed in bfloat16 or wider, within the bound.
No kernel may reach another device: no remote copies, remote signals or barrier semaphores. Data moves between devices by JAX's collectives and lax.ppermute only.
A program may use at most 128 MiB of HBM per device.

v0:
```python
import jax
import jax.numpy as jnp
from jax import lax
from jax.sharding import PartitionSpec as P

SITE_DEV = 512
TRACT_DEV = 1
TAXO = 128
G = 64
NB = 40


COEFFS = ((1.0, 1.1, 1.0, 6.0, 0.004, 0.6), (0.3, 1.4, 0.9, 8.0, 0.002, 0.7))
LOW_LEVEL = -6.0
LEVEL_STEP = 0.1


def intensity(geometry, coords, epsilon):
    start_x = geometry[0][:, None]
    start_y = geometry[1][:, None]
    along_x = (geometry[2] - geometry[0])[:, None]
    along_y = (geometry[3] - geometry[1])[:, None]
    rup_depth = geometry[4][:, None]
    magnitude = geometry[5][:, None]
    rel_x = coords[0][None, :] - start_x
    rel_y = coords[1][None, :] - start_y
    length_sq = along_x * along_x + along_y * along_y
    portion = jnp.clip((rel_x * along_x + rel_y * along_y) / length_sq, 0.0, 1.0)
    off_x = rel_x - portion * along_x
    off_y = rel_y - portion * along_y
    distance = jnp.sqrt(off_x * off_x + off_y * off_y + rup_depth * rup_depth)
    results = []
    for measure in range(2):
        coeffs = COEFFS[measure]
        value = (
            coeffs[0]
            + coeffs[1] * (magnitude - 6.0)
            - coeffs[2] * 0.5 * jnp.log(distance * distance + coeffs[3] * coeffs[3])
            - coeffs[4] * distance
            + coeffs[5] * epsilon[measure].astype(jnp.float32)
        )
        results.append(value)
    return jnp.stack(results)


def tent_weights(fields):
    position = jnp.clip((fields - LOW_LEVEL) / LEVEL_STEP, 0.0, G - 1.0)
    levels = jnp.arange(G, dtype=jnp.float32)
    weights = jnp.maximum(0.0, 1.0 - jnp.abs(position[..., None] - levels))
    n_events = fields.shape[1]
    n_sites = fields.shape[2]
    return weights.transpose(1, 2, 0, 3).reshape(n_events * n_sites, 2 * G).astype(jnp.bfloat16)


def curves(vulnerability, taxo_measure, taxo_offset):
    level_rows = jnp.arange(G, dtype=jnp.int32)[:, None] - taxo_offset[None, :]
    point_index = jnp.clip(level_rows, 0, NB - 1)
    curve_rows = jnp.take_along_axis(vulnerability.T, point_index, axis=0)
    blank = jnp.zeros_like(curve_rows)
    curve_rows = jnp.where(level_rows >= 0, curve_rows, blank)
    first_half = jnp.where(taxo_measure[None, :] == 0, curve_rows, blank)
    second_half = jnp.where(taxo_measure[None, :] == 1, curve_rows, blank)
    return jnp.concatenate([first_half, second_half], axis=0)


def build_exposure(asset_site, asset_taxo, asset_tract, asset_value, site_count, tracts):
    flat_index = (asset_taxo * site_count + asset_site) * tracts + asset_tract
    summed = jnp.zeros((TAXO * site_count * tracts,), jnp.float32).at[flat_index].add(asset_value)
    return summed.reshape(TAXO, site_count, tracts).astype(jnp.bfloat16)


def block_ratio(fields_block, curve_table):
    n_events = fields_block.shape[1]
    n_sites = fields_block.shape[2]
    loss_ratio = jnp.dot(
        tent_weights(fields_block), curve_table, preferred_element_type=jnp.float32
    )
    return loss_ratio.astype(jnp.bfloat16).reshape(n_events, n_sites, TAXO)


def all_terms(fields, curve_table, exposure):
    n_events = fields.shape[1]
    ev_block = min(32, n_events)
    tracts = exposure.shape[2]

    def loop_step(step_index, running):
        loss_ratio = block_ratio(fields, curve_table)
        term = jnp.einsum("bst,tsr->rbt", loss_ratio, exposure, preferred_element_type=jnp.float32)
        return term

    return lax.fori_loop(
        0, n_events // ev_block, loop_step, jnp.zeros((tracts, n_events, TAXO), jnp.float32)
    )


def shards(
    ruptures,
    event_rupture,
    epsilon,
    site_coords,
    vulnerability,
    taxo_measure,
    taxo_offset,
    asset_site,
    asset_taxo,
    asset_tract,
    asset_value,
):
    tracts = lax.axis_size("site") * TRACT_DEV
    rupture_rows = lax.all_gather(ruptures, ("ev", "site"), axis=1, tiled=True)
    geometry = jnp.take(rupture_rows, event_rupture, axis=1)
    event_fields = intensity(geometry, site_coords, epsilon)
    fields = lax.all_to_all(event_fields, "site", split_axis=2, concat_axis=1, tiled=True)
    curve_table = curves(vulnerability, taxo_measure, taxo_offset)
    exposure = build_exposure(asset_site, asset_taxo, asset_tract, asset_value, SITE_DEV, tracts)
    losses = lax.psum_scatter(
        all_terms(fields, curve_table, exposure), "site", scatter_dimension=0, tiled=True
    )
    return losses


def solution(mesh):
    in_specs = (
        P(None, ("ev", "site")),
        P(("ev", "site")),
        P(None, ("ev", "site"), None),
        P(),
        P(),
        P(),
        P(),
        P("site"),
        P("site"),
        P("site"),
        P("site"),
    )
    out_specs = P("site", "ev", None)
    return jax.shard_map(shards, mesh=mesh, in_specs=in_specs, out_specs=out_specs, check_vma=False)
```

profile of v0, /device:TPU:0, one launch (start us, length us, event | category | flops | bytes accessed | tf_op | source)
XLA Modules:
  0.0 267.0 jit_solution(6305388199920691578)
XLA Ops:
  0.0 0.0 copy-start
  0.7 43.5 %all-gather = f32[32,2,6]{2,1,0:T(2,128)S(1)} all-gather(f32[1,2,6]{2,1,0:T(2,128)} %bitcast.66), channel_id=1, replica_groups=mesh['ev'=4,'site'=8] {'ev','site'}, dimensions={0}, use_global_device_ids=true | all-gather | bytes 1584 | tf_op jit(solution)/shard_map/all_gather | solution.py:110
  44.2 0.7 fusion.23
  49.3 2.3 fusion.19
  51.6 0.8 fusion.18
  52.4 2.3 copy.32
  54.7 0.5 broadcast.227
  55.2 19.4 %reduce = f32[4096,2]{1,0:T(8,128)} reduce(f32[4096,1,2]{2,1,0:T(1,128)S(1)} %bitcast.59, f32[]{:T(128)} %broadcast.227), dimensions={1}, to_apply=%bitcast.51.reduce_sub_computation | reduce | bytes 65540
  74.6 3.7 %reshape.234 = f32[8,1,1024]{2,1,0:T(1,128)} reshape(f32[4096,2]{1,0:T(8,128)} %reduce) | data formatting | bytes 65536
  78.3 3.3 %all-to-all-start = ((f32[8,1,1024]{2,1,0:T(1,128)}), f32[8,1,1024]{2,1,0:T(1,128)S(1)}, u32[]{:S(2)}, u32[]{:S(2)}) async-start(f32[8,1,1024]{2,1,0:T(1,128)} %reshape.234), calls=%async_computation | async-start | bytes 65536 | tf_op jit(solution)/shard_map/all_to_all | solution.py:113
  81.7 0.0 copy-start.1
  81.7 0.0 copy-start.2
  81.7 0.0 copy-start.3
  81.7 65.6 %gather_fusion = bf16[8192]{0:T(1024)(128)(2,1)S(1)} fusion(bf16[40,128]{1,0:T(8,128)(2,1)S(1)} %bitcast.57, s32[8192]{0:T(1024)S(1)} %fusion.8), kind=kCustom, calls=%fused_computation | custom fusion | bytes 98304 | tf_op jit(solution)/shard_map/jit(take_along_axis)/gather | solution.py:58
  147.5 0.1 sub.156
  147.6 54.7 %scatter_custom_fusion = f32[524288]{0:T(1024)S(1)} fusion(s32[10240]{0:T(1024)S(1)} %compare_select_fusion, f32[10240]{0:T(1024)} %param.21, f32[]{:T(128)} %constant.32.clone.1), kind=kCustom, calls=%fused_computation.8 | custom fusion | flops 10240 | bytes 2097664 | tf_op jit(solution)/shard_map/scatter-add | solution.py:68
  202.3 0.1 convert_element_type.38
  202.4 0.0 copy-start.6
  202.5 20.0 %convert_element_type.39 = bf16[128,512,8]{2,1,0:T(8,128)(2,1)} reshape(bf16[524288]{0:T(1024)(128)(2,1)S(1)} %convert_element_type.38) | data formatting | bytes 2097152 | tf_op jit(solution)/shard_map/convert_element_type | solution.py:69
  222.5 0.6 dynamic-slice.5
  223.1 0.0 all-to-all-done
  223.1 0.7 reduce.1
  223.8 3.4 %reshape.235 = f32[4096,1,2]{2,1,0:T(1,128)S(1)} reshape(f32[8,1024]{1,0:T(8,128)S(1)} %reduce.1) | data formatting | bytes 65536
  227.2 1.9 copy.33
  229.2 0.2 sub.153
  229.5 1.6 copy.39
  231.1 0.6 convolution_convert_fusion
  231.7 0.9 copy.35
  232.6 8.2 %convolution_bitcast_fusion = f32[8,8,128]{1,0,2:T(8,128)S(1)} fusion(bf16[128,512,8]{2,1,0:T(8,128)(2,1)} %convert_element_type.39, bf16[8,512,128]{1,0,2:T(8,128)(2,1)S(1)} %copy.35), kind=kOutput, calls=%fused_computation.4 | convolution fusion | flops 8388608 | bytes 2129920 | tf_op jit(solution)/shard_map/while/body/eval_jaxpr/bst,tsr->rbt/dot_general | solution.py:88
  240.8 0.2 copy.36
  241.0 24.8 %all-reduce = f32[8,8,128]{2,1,0:T(8,128)S(1)} all-reduce(f32[8,8,128]{2,1,0:T(8,128)S(1)} %copy.36), channel_id=2, replica_groups=mesh['ev'=4,'site'=8] {'site'}, use_global_device_ids=true, to_apply=%region_1.2.clone | all-reduce | flops 8192 | bytes 65536
  265.8 1.2 constant_dynamic-slice_fusion
  (18 shorter events, 0.2 us)
Async XLA Ops:
  0.0 81.7 %copy-start = (bf16[128,40]{0,1:T(8,128)(2,1)S(1)}, bf16[128,40]{0,1:T(8,128)(2,1)}, u32[]{:S(2)}) copy-start(bf16[128,40]{0,1:T(8,128)(2,1)} %param.15) | copy-start | bytes 30724
  74.6 7.0 %copy-start.5 = (s32[128]{0:T(128)S(1)}, s32[128]{0:T(128)}, u32[]{:S(2)}) copy-start(s32[128]{0:T(128)} %param.16) | copy-start | bytes 1540
  74.6 7.0 %copy-start.4 = (s32[128]{0:T(128)S(1)}, s32[128]{0:T(128)}, u32[]{:S(2)}) copy-start(s32[128]{0:T(128)} %param.17) | copy-start | bytes 1540
  78.3 144.8 %all-to-all-start = ((f32[8,1,1024]{2,1,0:T(1,128)}), f32[8,1,1024]{2,1,0:T(1,128)S(1)}, u32[]{:S(2)}, u32[]{:S(2)}) async-start(f32[8,1,1024]{2,1,0:T(1,128)} %reshape.234), calls=%async_computation | async-start | bytes 65536 | tf_op jit(solution)/shard_map/all_to_all | solution.py:113
  81.7 65.7 %copy-start.1 = (s32[10240]{0:T(1024)S(1)}, s32[10240]{0:T(1024)}, u32[]{:S(2)}) copy-start(s32[10240]{0:T(1024)} %param.20) | copy-start | bytes 122884
  81.7 65.7 %copy-start.2 = (s32[10240]{0:T(1024)S(1)}, s32[10240]{0:T(1024)}, u32[]{:S(2)}) copy-start(s32[10240]{0:T(1024)} %param.18) | copy-start | bytes 122884
  81.7 65.7 %copy-start.3 = (s32[10240]{0:T(1024)S(1)}, s32[10240]{0:T(1024)}, u32[]{:S(2)}) copy-start(s32[10240]{0:T(1024)} %param.19) | copy-start | bytes 122884
  202.4 20.0 %copy-start.6 = (u32[32]{0:T(128)S(1)}, u32[32]{0:T(128)}, u32[]{:S(2)}) copy-start(u32[32]{0:T(128)} %constant.139) | copy-start | bytes 388
where the time goes:
time: 267 us
  local copies, waits for them, and re-layouts  103 us (39%)
  other arithmetic  78.2 us (29%)
  blocking collectives  68.3 us (26%)
  matrix products  8.75 us (3%)
  between operations  5.37 us (2%)
  starting transfers between devices  3.33 us (1%)
    gather x1, local copies, waits for them, and re-layouts, curves(): curve_rows = jnp.take_along_axis(vulnerability.T, point_index, axis=0)  65.6 us
    scatter-add x1, other arithmetic, build_exposure(): jnp.zeros((TAXO * site_count * tracts,), jnp.float32).at[flat_index]  54.7 us
    all_gather x1, blocking collectives, shards(): rupture_rows = lax.all_gather(ruptures, ('ev', 'site'), axis=1, tiled=True)  43.5 us
    unnamed x1, blocking collectives  24.8 us
    convert_element_type x1, local copies, waits for them, and re-layouts, build_exposure(): return summed.reshape(TAXO, site_count, tracts).astype(jnp.bfloat16)  20 us
    unnamed x1, other arithmetic  19.4 us
    unnamed x21, local copies, waits for them, and re-layouts  11.1 us
    dot_general x1, matrix products, loop_step(): jnp.einsum('bst,tsr->rbt', loss_ratio, exposure, preferred_element_type=j...  8.16 us
  transfers between devices with their start and end apart: 1, of which 0 were waited for; matrix products, arithmetic and copies ran while one was open for 53% of the time, Pallas kernels for 0%

commit v1 on v0

v1 whole, which is shorter than its diff:
```python
import jax
import jax.numpy as jnp
from jax import lax
from jax.experimental import pallas as pl
from jax.experimental.pallas import tpu as pltpu
from jax.sharding import PartitionSpec as P

SITE_DEV = 512
TAXO = 128
G = 64
NB = 40
LANES = 128
ROWS = 8

COEFFS = ((1.0, 1.1, 1.0, 6.0, 0.004, 0.6), (0.3, 1.4, 0.9, 8.0, 0.002, 0.7))
LOW_LEVEL = -6.0
LEVEL_STEP = 0.1

AXES = ("ev", "site")
F32 = jnp.float32
BF16 = jnp.bfloat16
NT = (((1,), (1,)), ((), ()))

VMEM = pl.BlockSpec(memory_space=pltpu.VMEM)
SMEM = pl.BlockSpec(memory_space=pltpu.SMEM)


def params():
    return pltpu.CompilerParams(vmem_limit_bytes=40 << 20)


def pack_kernel(n_ev, n_site, rup_ref, idx_ref, eps_ref, out_ref):
    n_rup = rup_ref.shape[1]
    lane = lax.broadcasted_iota(jnp.int32, (2, LANES), 1)
    row = jnp.zeros((2, LANES), F32)
    for b in range(n_rup):
        for c in range(6):
            row = jnp.where(lane == 6 * b + c, rup_ref[c, b], row)
    row = jnp.where(lane == 6 * n_rup, idx_ref[0].astype(F32), row)
    eps = eps_ref[...].astype(F32)

    def fill(i, carry):
        for j in range(n_site):
            out_ref[i * n_site + j, :, :SITE_DEV] = eps[:, j * SITE_DEV : (j + 1) * SITE_DEV]
            out_ref[i * n_site + j, :, SITE_DEV:] = row
        return carry

    lax.fori_loop(0, n_ev, fill, 0, unroll=n_ev <= 4)


def exposure_kernel(
    t_dev, rows, site_ref, taxo_ref, tract_ref, value_ref, vul_ref, measure_ref, offset_ref,
    exp_ref, curve_ref, site_s, col_s, high_s, low_s, sum_s, curve_s,
):
    me = lax.axis_index("ev")
    first = me * t_dev
    taxo = taxo_ref[...] - first
    own = (taxo >= 0) & (taxo < t_dev)
    value = value_ref[...]
    high = value.astype(BF16).astype(F32)
    site_s[...] = site_ref[...].astype(F32)
    col_s[...] = jnp.where(own, tract_ref[...] * t_dev + taxo, -1).astype(F32)
    high_s[...] = high
    low_s[...] = value - high

    n_col = exp_ref.shape[1]
    level = lax.broadcasted_iota(jnp.int32, (256, LANES), 0).astype(F32).astype(BF16)
    zero = jnp.zeros((256, LANES), BF16)
    one = jnp.ones((256, LANES), BF16)

    def spread(ref, q, less=0.0):
        return jnp.broadcast_to((ref[pl.ds(q, 1), :] - less).astype(BF16), (256, LANES))

    def beside(parts):
        return jnp.concatenate(parts, axis=1)

    sum_s[...] = jnp.zeros_like(sum_s)

    def step(c, carry):
        site_rows = [[] for _ in range(SITE_DEV // 256)]
        high_rows, low_rows = [], []
        for u in range(rows):
            q = c * rows + u
            for part, found in enumerate(site_rows):
                found.append(jnp.where(level == spread(site_s, q, 256.0 * part), one, zero))
            here = level == spread(col_s, q)
            high_rows.append(jnp.where(here, spread(high_s, q), zero))
            low_rows.append(jnp.where(here, spread(low_s, q), zero))
        at_site = jnp.concatenate([beside(found) for found in site_rows], axis=0)
        sum_s[...] += lax.dot_general(
            beside([at_site, at_site]), beside(high_rows + low_rows), NT, preferred_element_type=F32
        )
        return carry

    lax.fori_loop(0, site_s.shape[0] // rows, step, 0)
    exp_ref[...] = sum_s[...].astype(BF16)

    vul = vul_ref[...].astype(F32)
    table = jnp.concatenate([vul, jnp.broadcast_to(vul[NB - 1 : NB], (G - NB, TAXO))], axis=0)
    offset = jnp.broadcast_to(offset_ref[...], (G, TAXO))
    level_row = lax.broadcasted_iota(jnp.int32, (G, TAXO), 0)
    for bit in range(5):
        size = 1 << bit
        moved = jnp.where(level_row >= size, pltpu.roll(table, size, 0), 0.0)
        table = jnp.where((offset & size) != 0, moved, table)
    measure = jnp.broadcast_to(measure_ref[...], (G, TAXO))
    both = jnp.concatenate(
        [jnp.where(measure == 0, table, 0.0), jnp.where(measure == 1, table, 0.0)], axis=0
    )
    curve_s[...] = both.T
    curve_ref[...] = curve_s[pl.ds(pl.multiple_of(first, ROWS), t_dev), :].astype(BF16)


def swap_groups(block, groups, width):
    total = block.shape[0]
    high = total // groups
    row_group = lax.broadcasted_iota(jnp.int32, block.shape, 0) // high
    lane_group = lax.broadcasted_iota(jnp.int32, block.shape, 1) // width
    result = block
    for d in range(1, groups):
        moved = pltpu.roll(pltpu.roll(block, total - high * d, 0), width * d, 1)
        gap = lane_group - row_group
        result = jnp.where((gap == d) | (gap == d - groups), moved, result)
    return result


def loss_kernel(n_ev, n_site, n_rup, got_ref, coords_ref, exp_ref, curve_ref, out_ref, geo_s, ratio_s, loss_s):
    n_dev = n_ev * n_site
    t_dev = curve_ref.shape[0]
    n_col = exp_ref.shape[1]
    events = n_dev
    ev_dev = events // n_ev
    me = lax.axis_index("site")
    start = pl.multiple_of(me * SITE_DEV, LANES)
    x = jnp.broadcast_to(coords_ref[0:1, pl.ds(start, SITE_DEV)], (ROWS, SITE_DEV))
    y = jnp.broadcast_to(coords_ref[1:2, pl.ds(start, SITE_DEV)], (ROWS, SITE_DEV))

    def take_geometry(b, carry):
        rows = [got_ref[b * ROWS + u, :, SITE_DEV:][0:1] for u in range(ROWS)]
        geo_s[pl.ds(pl.multiple_of(b * ROWS, ROWS), ROWS), :] = jnp.concatenate(rows, axis=0)
        return carry

    lax.fori_loop(0, n_dev // ROWS, take_geometry, 0, unroll=n_dev // ROWS <= 4)
    every = geo_s[...]
    high = every.astype(BF16)
    rest = every - high.astype(F32)
    middle = rest.astype(BF16)
    low = (rest - middle.astype(F32)).astype(BF16)
    level = lax.broadcasted_iota(jnp.int32, (G, SITE_DEV), 0).astype(F32).astype(BF16)
    level_less = (lax.broadcasted_iota(jnp.int32, (G, SITE_DEV), 0) - 1).astype(F32).astype(BF16)
    zero = jnp.zeros((G, SITE_DEV), BF16)
    curve = curve_ref[...]
    exposure = exp_ref[...]
    diagonal = lax.broadcasted_iota(jnp.int32, (t_dev, n_col), 0) == (
        lax.broadcasted_iota(jnp.int32, (t_dev, n_col), 1) % t_dev
    )

    def block(b, carry):
        first = pl.multiple_of(b * ROWS, ROWS)
        rupture = geo_s[pl.ds(first, ROWS), :][:, 6 * n_rup : 6 * n_rup + 1].astype(jnp.int32)
        owner = rupture // n_rup
        hot = (lax.broadcasted_iota(jnp.int32, (ROWS, n_dev), 1) == owner).astype(BF16)
        found = (
            jnp.dot(hot, high, preferred_element_type=F32)
            + jnp.dot(hot, middle, preferred_element_type=F32)
        ) + jnp.dot(hot, low, preferred_element_type=F32)
        own = found
        for u in range(1, n_rup):
            own = jnp.where(rupture - owner * n_rup == u, pltpu.roll(found, LANES - 6 * u, 1), own)
        start_x = own[:, 0:1]
        start_y = own[:, 1:2]
        along_x = own[:, 2:3] - start_x
        along_y = own[:, 3:4] - start_y
        depth = own[:, 4:5]
        size = own[:, 5:6]
        length_sq = along_x * along_x + along_y * along_y
        rel_x = x - start_x
        rel_y = y - start_y
        portion = jnp.clip((rel_x * along_x + rel_y * along_y) / length_sq, 0.0, 1.0)
        off_x = rel_x - portion * along_x
        off_y = rel_y - portion * along_y
        squared = off_x * off_x + off_y * off_y + depth * depth
        distance = jnp.sqrt(squared)
        got = [got_ref[b * ROWS + u, :, :SITE_DEV] for u in range(ROWS)]
        below, weight_0, weight_1 = [], [], []
        for k in range(2):
            c = COEFFS[k]
            eps = jnp.concatenate([rows[k : k + 1] for rows in got], axis=0)
            field = (
                c[0] + c[1] * (size - 6.0)
                - c[2] * 0.5 * jnp.log(distance * distance + c[3] * c[3])
                - c[4] * distance
                + c[5] * eps
            )
            position = jnp.clip((field - LOW_LEVEL) / LEVEL_STEP, 0.0, G - 1.0)
            floor = jnp.floor(position)
            below.append(floor)
            weight_0.append(1.0 - (position - floor))
            weight_1.append(jnp.maximum(0.0, 1.0 - ((floor + 1.0) - position)))

        def wide(array, e):
            return jnp.broadcast_to(array[e : e + 1].astype(BF16), (G, SITE_DEV))

        for e in range(ROWS):
            tents = []
            for k in range(2):
                at = wide(below[k], e)
                tents.append(
                    jnp.where(
                        level == at,
                        wide(weight_0[k], e),
                        jnp.where(level_less == at, wide(weight_1[k], e), zero),
                    )
                )
            ratio = jnp.dot(curve, jnp.concatenate(tents, axis=0), preferred_element_type=F32)
            ratio_s[e * t_dev : (e + 1) * t_dev, :] = ratio
        terms = jnp.dot(ratio_s[...].astype(BF16), exposure, preferred_element_type=F32)
        rows = [
            jnp.sum(jnp.where(diagonal, terms[e * t_dev : (e + 1) * t_dev], 0.0), axis=0, keepdims=True)
            for e in range(ROWS)
        ]
        loss_s[pl.ds(first, ROWS), :] = jnp.concatenate(rows, axis=0)
        return carry

    lax.fori_loop(0, events // ROWS, block, 0)

    halves = n_col // LANES

    def arrange(i, carry):
        first = pl.multiple_of(i * ev_dev, ROWS)
        for u in range(halves):
            part = loss_s[pl.ds(first, ev_dev), u * LANES : (u + 1) * LANES]
            out_ref[pl.ds(pl.multiple_of((i * halves + u) * ev_dev, ROWS), ev_dev), :] = swap_groups(
                part, n_ev, t_dev
            )
        return carry

    lax.fori_loop(0, n_ev, arrange, 0, unroll=n_ev <= 4)


def total_kernel(n_ev, n_site, got_ref, out_ref):
    high = got_ref.shape[0] // (n_ev * n_site)
    rows = []
    for i in range(n_ev):
        for h in range(high):
            part = got_ref[pl.ds(i * n_site * high + h, n_site, stride=high), :]
            rows.append(jnp.sum(part, axis=0, keepdims=True))
    out_ref[...] = swap_groups(jnp.concatenate(rows, axis=0), n_ev, LANES // n_ev)


def shards(
    ruptures,
    event_rupture,
    epsilon,
    site_coords,
    vulnerability,
    taxo_measure,
    taxo_offset,
    asset_site,
    asset_taxo,
    asset_tract,
    asset_value,
):
    n_ev = lax.axis_size("ev")
    n_site = lax.axis_size("site")
    n_dev = n_ev * n_site
    n_rup = ruptures.shape[1]
    sites = epsilon.shape[2]
    t_dev = TAXO // n_ev
    n_col = n_site * t_dev
    asset_rows = asset_site.shape[0] // LANES

    def exchange(array):
        return lax.all_to_all(array, AXES, split_axis=0, concat_axis=0, tiled=True)

    packed = pl.pallas_call(
        lambda *refs: pack_kernel(n_ev, n_site, *refs),
        out_shape=jax.ShapeDtypeStruct((n_dev, 2, SITE_DEV + LANES), F32),
        in_specs=[SMEM, SMEM, VMEM],
        out_specs=VMEM,
        compiler_params=params(),
    )(ruptures, event_rupture, epsilon.reshape(2, sites))
    got = exchange(packed)

    def as_rows(array):
        return array.reshape(asset_rows, LANES)

    exposure, curve = pl.pallas_call(
        lambda *refs: exposure_kernel(t_dev, 20, *refs),
        out_shape=(
            jax.ShapeDtypeStruct((SITE_DEV, n_col), BF16),
            jax.ShapeDtypeStruct((t_dev, 2 * G), BF16),
        ),
        in_specs=[VMEM] * 7,
        out_specs=(VMEM, VMEM),
        scratch_shapes=[pltpu.VMEM((asset_rows, LANES), F32)] * 4
        + [pltpu.VMEM((SITE_DEV, n_col), F32), pltpu.VMEM((TAXO, 2 * G), F32)],
        compiler_params=params(),
        cost_estimate=pl.CostEstimate(
            flops=4 * asset_rows * LANES * SITE_DEV * n_col, bytes_accessed=1 << 20, transcendentals=0
        ),
    )(
        as_rows(asset_site),
        as_rows(asset_taxo),
        as_rows(asset_tract),
        as_rows(asset_value),
        vulnerability.T,
        taxo_measure.reshape(1, TAXO),
        taxo_offset.reshape(1, TAXO),
    )

    parts = pl.pallas_call(
        lambda *refs: loss_kernel(n_ev, n_site, n_rup, *refs),
        out_shape=jax.ShapeDtypeStruct((n_dev * n_col // LANES, LANES), F32),
        in_specs=[VMEM] * 4,
        out_specs=VMEM,
        scratch_shapes=[
            pltpu.VMEM((n_dev, LANES), F32),
            pltpu.VMEM((ROWS * t_dev, SITE_DEV), F32),
            pltpu.VMEM((n_dev, n_col), F32),
        ],
        compiler_params=params(),
    )(got, site_coords, exposure, curve)

    losses = pl.pallas_call(
        lambda *refs: total_kernel(n_ev, n_site, *refs),
        out_shape=jax.ShapeDtypeStruct((n_dev // n_ev, LANES), F32),
        in_specs=[VMEM],
        out_specs=VMEM,
        compiler_params=params(),
    )(exchange(parts))
    return losses[None]


def solution(mesh):
    in_specs = (
        P(None, ("ev", "site")),
        P(("ev", "site")),
        P(None, ("ev", "site"), None),
        P(),
        P(),
        P(),
        P(),
        P("site"),
        P("site"),
        P("site"),
        P("site"),
    )
    out_specs = P("site", "ev", None)
    return jax.shard_map(shards, mesh=mesh, in_specs=in_specs, out_specs=out_specs, check_vma=False)
```

time: 267 us -> 35.2 us (0.13)
  local copies, waits for them, and re-layouts: 103 us -> 1.49 us
  other arithmetic: 78.2 us -> 0 us
  blocking collectives: 68.3 us -> 11.5 us
  Pallas kernels: 0 us -> 12.3 us
  matrix products: 8.75 us -> 0 us
  between operations: 5.37 us -> 0.76 us
  starting transfers between devices: 3.33 us -> 7.3 us
    gather x1 -> x0, local copies, waits for them, and re-layouts: 65.6 us -> none  [curves(): curve_rows = jnp.take_along_axis(vulnerability.T, point_index, axis=0)]
    scatter-add x1 -> x0, other arithmetic: 54.7 us -> none  [build_exposure(): jnp.zeros((TAXO * site_count * tracts,), jnp.float32).at[flat_index]]
    all_gather x1 -> x0, blocking collectives: 43.5 us -> none  [shards(): rupture_rows = lax.all_gather(ruptures, ('ev', 'site'), axis=1, tiled=True)]
    unnamed x1 -> x0, blocking collectives: 24.8 us -> none
    convert_element_type x1 -> x0, local copies, waits for them, and re-layouts: 20 us -> none  [build_exposure(): return summed.reshape(TAXO, site_count, tracts).astype(jnp.bfloat16)]
    unnamed x1 -> x0, other arithmetic: 19.4 us -> none
    pallas_call x0 -> x4, Pallas kernels: none -> 12.3 us  [the longest x1 6.4 us: shards(): pl.pallas_call(lambda *refs: exposure_kernel(t_dev, 20, *refs), out_shape...]
    all_to_all x0 -> x1, blocking collectives: none -> 11.5 us  [exchange(): return lax.all_to_all(array, AXES, split_axis=0, concat_axis=0, tiled=True)]
  transfers between devices with their start and end apart: 1 -> 1, of which waited for: 0 -> 1; matrix products, arithmetic and copies ran while one was open for 53% -> 0% of each run, Pallas kernels for 0% -> 18%
where the time goes in v1:
time: 35.2 us; the launch traced here: 34.8 us
  Pallas kernels  12.3 us (35%)
  blocking collectives  11.5 us (33%)
  starting transfers between devices  7.3 us (21%)
  local copies, waits for them, and re-layouts  1.49 us (4%)
  waiting for transfers between devices  1.45 us (4%)
  between operations  0.76 us (2%)
    all_to_all x1, blocking collectives, exchange(): return lax.all_to_all(array, AXES, split_axis=0, concat_axis=0, tiled=True)  11.5 us
    all_to_all x1, starting transfers between devices, exchange(): return lax.all_to_all(array, AXES, split_axis=0, concat_axis=0, tiled=True)  7.3 us
    pallas_call x1, Pallas kernels, shards(): pl.pallas_call(lambda *refs: exposure_kernel(t_dev, 20, *refs), out_shape...  6.4 us
    pallas_call x1, Pallas kernels, shards(): pl.pallas_call(lambda *refs: loss_kernel(n_ev, n_site, n_rup, *refs), out...  3.99 us
    unnamed x21, local copies, waits for them, and re-layouts  1.49 us
    all_to_all x1, waiting for transfers between devices, exchange(): return lax.all_to_all(array, AXES, split_axis=0, concat_axis=0, tiled=True)  1.45 us
    pallas_call x1, Pallas kernels, shards(): pl.pallas_call(lambda *refs: pack_kernel(n_ev, n_site, *refs), out_shape=...  1.28 us
  transfers between devices with their start and end apart: 1, of which 1 were waited for; matrix products, arithmetic and copies ran while one was open for 0% of the time, Pallas kernels for 18%

profile of v1, /device:TPU:0, one launch (start us, length us, event | category | flops | bytes accessed | tf_op | source)
XLA Modules:
  0.0 34.8 jit_solution(15802790078446025311)
XLA Ops:
  0.0 0.0 copy-start.9
  0.7 0.0 copy-done.9
  0.7 0.1 copy.12.refs_0_
  0.8 0.0 copy-start.1
  0.8 0.7 %copy-done.1 = bf16[2,1,4096]{2,0,1:T(2,128)(2,1)S(1)} copy-done((bf16[2,1,4096]{2,0,1:T(2,128)(2,1)S(1)}, bf16[2,1,4096]{2,0,1:T(2,128)(2,1)}, u32[]{:S(2)}) %copy-start.1) | copy-done | bytes 16408
  1.5 1.3 %shard_map.109 = f32[32,2,640]{2,1,0:T(2,128)} custom-call(f32[6,2]{1,0:T(8,128)S(1)} %copy.12.refs_0_, s32[1]{0:T(128)S(6)} %copy.13.refs_1_, bf16[2,4096]{1,0:T(2,128)(2,1)S(1)} %bitcast.13), custom_call_target="tpu_custom_call" | custom-call | tf_op jit(solution)/shard_map/pallas_call | solution.py:276
  2.8 0.0 copy-start.2
  2.8 0.0 copy-start.3
  2.8 0.0 copy-start.4
  2.8 0.0 copy-start.5
  2.8 7.3 %all-to-all-start = ((f32[32,2,640]{2,1,0:T(2,128)}), f32[32,2,640]{2,1,0:T(2,128)S(1)}, u32[]{:S(2)}, u32[]{:S(2)}) async-start(f32[32,2,640]{2,1,0:T(2,128)} %shard_map.109), calls=%async_computation | async-start | bytes 327680 | tf_op jit(solution)/shard_map/all_to_all | solution.py:274
  10.1 0.0 copy-start.6
  10.1 0.0 copy-start.7
  10.1 0.0 copy-start.8
  10.1 0.0 copy-done.2
  10.1 0.0 copy-done.3
  10.2 0.0 copy-done.4
  10.2 0.0 copy-done.5
  10.2 0.6 %copy-done.6 = bf16[128,40]{0,1:T(8,128)(2,1)S(1)} copy-done((bf16[128,40]{0,1:T(8,128)(2,1)S(1)}, bf16[128,40]{0,1:T(8,128)(2,1)}, u32[]{:S(2)}) %copy-start.6) | copy-done | bytes 10264
  10.8 0.0 copy-done.7
  10.8 0.0 copy-done.8
  10.8 0.0 copy-start
  10.8 6.4 %shard_map.110 = (bf16[512,256]{1,0:T(8,128)(2,1)S(1)}, bf16[32,128]{1,0:T(8,128)(2,1)S(1)}) custom-call(s32[80,128]{1,0:T(8,128)S(1)} %bitcast.14, s32[80,128]{1,0:T(8,128)S(1)} %bitcast.15, s32[80,128]{1,0:T(8,128)S(1)} %bitcast.16, f32[80,128]{1,0:T(8,128)S(1)} %bitcast.17, bf16[40,128]{1,0:T(8,128)(2,1)S(1)} %bitcast.18, s32[1,128]{1,0:T(1,128)S(1)} %bitcast.19, ...), custom_call_target="tpu_custom_call" | custom-call | flops 5368709120 | bytes 1048576 | tf_op jit(solution)/shard_map/pallas_call | solution.py:288
  17.2 1.5 %all-to-all-done.refs_0_ = f32[32,2,640]{2,1,0:T(2,128)S(1)} async-done(((f32[32,2,640]{2,1,0:T(2,128)}), f32[32,2,640]{2,1,0:T(2,128)S(1)}, u32[]{:S(2)}, u32[]{:S(2)}) %all-to-all-start) | async-done | bytes 163872 | tf_op jit(solution)/shard_map/all_to_all | solution.py:274
  18.7 0.0 copy-done
  18.7 4.0 %shard_map.111 = f32[64,128]{1,0:T(8,128)S(1)} custom-call(f32[32,2,640]{2,1,0:T(2,128)S(1)} %all-to-all-done.refs_0_, f32[2,4096]{1,0:T(2,128)S(1)} %copy-done, bf16[512,256]{1,0:T(8,128)(2,1)S(1)} %get-tuple-element.7.refs_2_, bf16[32,128]{1,0:T(8,128)(2,1)S(1)} %get-tuple-element.8.refs_3_), custom_call_target="tpu_custom_call" | custom-call | tf_op jit(solution)/shard_map/pallas_call | solution.py:312
  22.7 11.5 %all_to_all.16 = f32[32,2,128]{2,1,0:T(2,128)S(1)} all-to-all(f32[32,2,128]{2,1,0:T(2,128)S(1)} %bitcast.12), channel_id=1, replica_groups=mesh['ev'=4,'site'=8] {'ev','site'}, dimensions={0} | all-to-all | bytes 65536 | tf_op jit(solution)/shard_map/all_to_all | solution.py:274
  34.1 0.7 %shard_map.112 = f32[8,128]{1,0:T(8,128)} custom-call(f32[64,128]{1,0:T(8,128)S(1)} %bitcast.11), custom_call_target="tpu_custom_call" | custom-call | tf_op jit(solution)/shard_map/pallas_call | solution.py:325
Async XLA Ops:
  0.0 0.7 %copy-start.9 = (f32[6,2]{0,1:T(2,128)S(1)}, f32[6,2]{0,1:T(2,128)}, u32[]{:S(2)}) copy-start(f32[6,2]{0,1:T(2,128)} %param.11) | copy-start | bytes 148
  0.8 0.7 %copy-start.1 = (bf16[2,1,4096]{2,0,1:T(2,128)(2,1)S(1)}, bf16[2,1,4096]{2,0,1:T(2,128)(2,1)}, u32[]{:S(2)}) copy-start(bf16[2,1,4096]{2,0,1:T(2,128)(2,1)} %param.13) | copy-start | bytes 49156
  2.8 7.4 %copy-start.2 = (s32[10240]{0:T(1024)S(1)}, s32[10240]{0:T(1024)}, u32[]{:S(2)}) copy-start(s32[10240]{0:T(1024)} %param.18) | copy-start | bytes 122884
  2.8 7.4 %copy-start.3 = (s32[10240]{0:T(1024)S(1)}, s32[10240]{0:T(1024)}, u32[]{:S(2)}) copy-start(s32[10240]{0:T(1024)} %param.19) | copy-start | bytes 122884
  2.8 7.4 %copy-start.4 = (s32[10240]{0:T(1024)S(1)}, s32[10240]{0:T(1024)}, u32[]{:S(2)}) copy-start(s32[10240]{0:T(1024)} %param.20) | copy-start | bytes 122884
  2.8 7.4 %copy-start.5 = (f32[10240]{0:T(1024)S(1)}, f32[10240]{0:T(1024)}, u32[]{:S(2)}) copy-start(f32[10240]{0:T(1024)} %param.21) | copy-start | bytes 122884
  2.8 15.9 %all-to-all-start = ((f32[32,2,640]{2,1,0:T(2,128)}), f32[32,2,640]{2,1,0:T(2,128)S(1)}, u32[]{:S(2)}, u32[]{:S(2)}) async-start(f32[32,2,640]{2,1,0:T(2,128)} %shard_map.109), calls=%async_computation | async-start | bytes 327680 | tf_op jit(solution)/shard_map/all_to_all | solution.py:274
  10.1 0.7 %copy-start.6 = (bf16[128,40]{0,1:T(8,128)(2,1)S(1)}, bf16[128,40]{0,1:T(8,128)(2,1)}, u32[]{:S(2)}) copy-start(bf16[128,40]{0,1:T(8,128)(2,1)} %param.15) | copy-start | bytes 30724
  10.1 0.7 %copy-start.7 = (s32[128]{0:T(128)S(1)}, s32[128]{0:T(128)}, u32[]{:S(2)}) copy-start(s32[128]{0:T(128)} %param.16) | copy-start | bytes 1540
  10.1 0.7 %copy-start.8 = (s32[128]{0:T(128)S(1)}, s32[128]{0:T(128)}, u32[]{:S(2)}) copy-start(s32[128]{0:T(128)} %param.17) | copy-start | bytes 1540
  10.8 7.9 %copy-start = (f32[2,4096]{1,0:T(2,128)S(1)}, f32[2,4096]{1,0:T(2,128)}, u32[]{:S(2)}) copy-start(f32[2,4096]{1,0:T(2,128)} %refs_1_.2) | copy-start | bytes 98308

commit v2 on v1

--- a/solution.py
+++ b/solution.py
@@ -11,6 +11,12 @@
 NB = 40
 LANES = 128
 ROWS = 8
+PART = 16
+EVENT_BLOCK = 32
+CODES = 1 << 17
+SLANT = 13
+HOLE = 1 << 24
+COMPACT_ROWS = 16
 
 COEFFS = ((1.0, 1.1, 1.0, 6.0, 0.004, 0.6), (0.3, 1.4, 0.9, 8.0, 0.002, 0.7))
 LOW_LEVEL = -6.0
@@ -22,22 +28,40 @@
 NT = (((1,), (1,)), ((), ()))
 
 VMEM = pl.BlockSpec(memory_space=pltpu.VMEM)
-SMEM = pl.BlockSpec(memory_space=pltpu.SMEM)
-
-
-def params():
-    return pltpu.CompilerParams(vmem_limit_bytes=40 << 20)
-
-
-def pack_kernel(n_ev, n_site, rup_ref, idx_ref, eps_ref, out_ref):
-    n_rup = rup_ref.shape[1]
+HBM = pl.BlockSpec(memory_space=pltpu.HBM)
+
+
+def params(mebibytes):
+    return pltpu.CompilerParams(vmem_limit_bytes=mebibytes << 20)
+
+
+def parts_of(value):
+    high = value.astype(BF16).astype(F32)
+    rest = value - high
+    middle = rest.astype(BF16).astype(F32)
+    return high, middle, (rest - middle).astype(BF16).astype(F32)
+
+
+def pack_kernel(n_ev, n_site, rup_hbm, idx_hbm, eps_hbm, out_ref, rup_ref, idx_ref, eps_ref, sems):
+    copies = [
+        pltpu.make_async_copy(source, target, sems.at[k])
+        for k, (source, target) in enumerate(((rup_hbm, rup_ref), (idx_hbm, idx_ref), (eps_hbm, eps_ref)))
+    ]
+    for copy in copies:
+        copy.start()
+    n_rup = rup_ref.shape[0]
     lane = lax.broadcasted_iota(jnp.int32, (2, LANES), 1)
     row = jnp.zeros((2, LANES), F32)
+    copies[0].wait()
+    copies[1].wait()
     for b in range(n_rup):
         for c in range(6):
-            row = jnp.where(lane == 6 * b + c, rup_ref[c, b], row)
+            row = jnp.where(lane == 6 * b + c, rup_ref[b, c], row)
     row = jnp.where(lane == 6 * n_rup, idx_ref[0].astype(F32), row)
-    eps = eps_ref[...].astype(F32)
+    high, middle, low = parts_of(row)
+    row = (high + pltpu.roll(middle, PART, 1) + pltpu.roll(low, 2 * PART, 1)).astype(BF16)
+    copies[2].wait()
+    eps = eps_ref[...]
 
     def fill(i, carry):
         for j in range(n_site):
@@ -48,22 +72,62 @@
     lax.fori_loop(0, n_ev, fill, 0, unroll=n_ev <= 4)
 
 
+def compact(own, code, value):
+    rows = own.shape[0]
+    above = lax.broadcasted_iota(jnp.int32, (rows, rows), 1) < lax.broadcasted_iota(jnp.int32, (rows, rows), 0)
+    gaps = jnp.dot(above.astype(BF16), 1.0 - own.astype(BF16), preferred_element_type=F32).astype(jnp.int32)
+    word = jnp.where(own, gaps * CODES + code, HOLE)
+    size = 1
+    while size < rows:
+        bit = size * CODES
+        from_word = jnp.concatenate([word[size:], jnp.full((size, LANES), HOLE, jnp.int32)], axis=0)
+        from_value = jnp.concatenate([value[size:], jnp.zeros((size, LANES), F32)], axis=0)
+        comes = (from_word & bit) != 0
+        value = jnp.where(comes, from_value, value)
+        word = jnp.where(comes, from_word, jnp.where((word & bit) != 0, HOLE, word))
+        size *= 2
+    return word, value
+
+
+def slanted(array):
+    return jnp.concatenate(
+        [
+            pltpu.roll(array[q : q + ROWS], (11 * q // ROWS) % 36, 1, stride=SLANT, stride_axis=0)
+            for q in range(0, array.shape[0], ROWS)
+        ],
+        axis=0,
+    )
+
+
 def exposure_kernel(
-    t_dev, rows, site_ref, taxo_ref, tract_ref, value_ref, vul_ref, measure_ref, offset_ref,
-    exp_ref, curve_ref, site_s, col_s, high_s, low_s, sum_s, curve_s,
+    t_dev, rows, site_ref, taxo_ref, tract_ref, value_ref, vul_hbm, measure_hbm, offset_hbm,
+    exp_ref, curve_ref, site_s, col_s, high_s, low_s, sum_s, curve_s, vul_ref, measure_ref, offset_ref, sems,
 ):
+    copies = [
+        pltpu.make_async_copy(source, target, sems.at[k])
+        for k, (source, target) in enumerate(
+            ((vul_hbm, vul_ref), (measure_hbm, measure_ref), (offset_hbm, offset_ref))
+        )
+    ]
+    for copy in copies:
+        copy.start()
     me = lax.axis_index("ev")
     first = me * t_dev
+    n_col = exp_ref.shape[1]
     taxo = taxo_ref[...] - first
     own = (taxo >= 0) & (taxo < t_dev)
-    value = value_ref[...]
+    code = site_ref[...] * n_col + tract_ref[...] * t_dev + taxo
+    word, value = compact(own, code, value_ref[...])
+    word, value = slanted(word), slanted(value)
+    own = word != HOLE
+    most = jnp.max(jnp.sum(own.astype(F32), axis=0, keepdims=True)).astype(jnp.int32)
+    word, value = compact(own, word & (CODES - 1), value)
     high = value.astype(BF16).astype(F32)
-    site_s[...] = site_ref[...].astype(F32)
-    col_s[...] = jnp.where(own, tract_ref[...] * t_dev + taxo, -1).astype(F32)
+    site_s[...] = ((word & (CODES - 1)) // n_col).astype(F32)
+    col_s[...] = jnp.where((word & HOLE) != 0, -1, word & (n_col - 1)).astype(F32)
     high_s[...] = high
     low_s[...] = value - high
 
-    n_col = exp_ref.shape[1]
     level = lax.broadcasted_iota(jnp.int32, (256, LANES), 0).astype(F32).astype(BF16)
     zero = jnp.zeros((256, LANES), BF16)
     one = jnp.ones((256, LANES), BF16)
@@ -92,9 +156,11 @@
         )
         return carry
 
-    lax.fori_loop(0, site_s.shape[0] // rows, step, 0)
+    lax.fori_loop(0, (most + rows - 1) // rows, step, 0)
     exp_ref[...] = sum_s[...].astype(BF16)
 
+    for copy in copies:
+        copy.wait()
     vul = vul_ref[...].astype(F32)
     table = jnp.concatenate([vul, jnp.broadcast_to(vul[NB - 1 : NB], (G - NB, TAXO))], axis=0)
     offset = jnp.broadcast_to(offset_ref[...], (G, TAXO))
@@ -132,20 +198,17 @@
     ev_dev = events // n_ev
     me = lax.axis_index("site")
     start = pl.multiple_of(me * SITE_DEV, LANES)
-    x = jnp.broadcast_to(coords_ref[0:1, pl.ds(start, SITE_DEV)], (ROWS, SITE_DEV))
-    y = jnp.broadcast_to(coords_ref[1:2, pl.ds(start, SITE_DEV)], (ROWS, SITE_DEV))
+    x = coords_ref[0:1, pl.ds(start, SITE_DEV)]
+    y = coords_ref[1:2, pl.ds(start, SITE_DEV)]
 
     def take_geometry(b, carry):
-        rows = [got_ref[b * ROWS + u, :, SITE_DEV:][0:1] for u in range(ROWS)]
-        geo_s[pl.ds(pl.multiple_of(b * ROWS, ROWS), ROWS), :] = jnp.concatenate(rows, axis=0)
+        first = b * EVENT_BLOCK
+        rows = [got_ref[first + u, :, SITE_DEV:].astype(F32)[0:1] for u in range(EVENT_BLOCK)]
+        geo_s[pl.ds(pl.multiple_of(first, ROWS), EVENT_BLOCK), :] = jnp.concatenate(rows, axis=0)
         return carry
 
-    lax.fori_loop(0, n_dev // ROWS, take_geometry, 0, unroll=n_dev // ROWS <= 4)
-    every = geo_s[...]
-    high = every.astype(BF16)
-    rest = every - high.astype(F32)
-    middle = rest.astype(BF16)
-    low = (rest - middle.astype(F32)).astype(BF16)
+    lax.fori_loop(0, n_dev // EVENT_BLOCK, take_geometry, 0)
+    ruptures = geo_s[...].astype(BF16)
     level = lax.broadcasted_iota(jnp.int32, (G, SITE_DEV), 0).astype(F32).astype(BF16)
     level_less = (lax.broadcasted_iota(jnp.int32, (G, SITE_DEV), 0) - 1).astype(F32).astype(BF16)
     zero = jnp.zeros((G, SITE_DEV), BF16)
@@ -155,15 +218,16 @@
         lax.broadcasted_iota(jnp.int32, (t_dev, n_col), 1) % t_dev
     )
 
+    def joined(array):
+        return (array + pltpu.roll(array, LANES - PART, 1)) + pltpu.roll(array, LANES - 2 * PART, 1)
+
     def block(b, carry):
-        first = pl.multiple_of(b * ROWS, ROWS)
-        rupture = geo_s[pl.ds(first, ROWS), :][:, 6 * n_rup : 6 * n_rup + 1].astype(jnp.int32)
+        first = pl.multiple_of(b * EVENT_BLOCK, EVENT_BLOCK)
+        here = joined(geo_s[pl.ds(first, EVENT_BLOCK), :])
+        rupture = here[:, 6 * n_rup : 6 * n_rup + 1].astype(jnp.int32)
         owner = rupture // n_rup
-        hot = (lax.broadcasted_iota(jnp.int32, (ROWS, n_dev), 1) == owner).astype(BF16)
-        found = (
-            jnp.dot(hot, high, preferred_element_type=F32)
-            + jnp.dot(hot, middle, preferred_element_type=F32)
-        ) + jnp.dot(hot, low, preferred_element_type=F32)
+        hot = (lax.broadcasted_iota(jnp.int32, (EVENT_BLOCK, n_dev), 1) == owner).astype(BF16)
+        found = joined(jnp.dot(hot, ruptures, preferred_element_type=F32))
         own = found
         for u in range(1, n_rup):
             own = jnp.where(rupture - owner * n_rup == u, pltpu.roll(found, LANES - 6 * u, 1), own)
@@ -179,9 +243,8 @@
         portion = jnp.clip((rel_x * along_x + rel_y * along_y) / length_sq, 0.0, 1.0)
         off_x = rel_x - portion * along_x
         off_y = rel_y - portion * along_y
-        squared = off_x * off_x + off_y * off_y + depth * depth
-        distance = jnp.sqrt(squared)
-        got = [got_ref[b * ROWS + u, :, :SITE_DEV] for u in range(ROWS)]
+        distance = jnp.sqrt(off_x * off_x + off_y * off_y + depth * depth)
+        got = [got_ref[b * EVENT_BLOCK + u, :, :SITE_DEV].astype(F32) for u in range(EVENT_BLOCK)]
         below, weight_0, weight_1 = [], [], []
         for k in range(2):
             c = COEFFS[k]
@@ -201,7 +264,8 @@
         def wide(array, e):
             return jnp.broadcast_to(array[e : e + 1].astype(BF16), (G, SITE_DEV))
 
-        for e in range(ROWS):
+        ratios = []
+        for e in range(EVENT_BLOCK):
             tents = []
             for k in range(2):
                 at = wide(below[k], e)
@@ -213,16 +277,19 @@
                     )
                 )
             ratio = jnp.dot(curve, jnp.concatenate(tents, axis=0), preferred_element_type=F32)
-            ratio_s[e * t_dev : (e + 1) * t_dev, :] = ratio
-        terms = jnp.dot(ratio_s[...].astype(BF16), exposure, preferred_element_type=F32)
+            ratios.append(ratio.astype(BF16))
+            if len(ratios) * t_dev == 32:
+                ratio_s[(e + 1) * t_dev - 32 : (e + 1) * t_dev, :] = jnp.concatenate(ratios, axis=0)
+                ratios = []
+        terms = jnp.dot(ratio_s[...], exposure, preferred_element_type=F32)
         rows = [
             jnp.sum(jnp.where(diagonal, terms[e * t_dev : (e + 1) * t_dev], 0.0), axis=0, keepdims=True)
-            for e in range(ROWS)
+            for e in range(EVENT_BLOCK)
         ]
-        loss_s[pl.ds(first, ROWS), :] = jnp.concatenate(rows, axis=0)
+        loss_s[pl.ds(first, EVENT_BLOCK), :] = jnp.concatenate(rows, axis=0)
         return carry
 
-    lax.fori_loop(0, events // ROWS, block, 0)
+    lax.fori_loop(0, events // EVENT_BLOCK, block, 0)
 
     halves = n_col // LANES
 
@@ -275,29 +342,37 @@
 
     packed = pl.pallas_call(
         lambda *refs: pack_kernel(n_ev, n_site, *refs),
-        out_shape=jax.ShapeDtypeStruct((n_dev, 2, SITE_DEV + LANES), F32),
-        in_specs=[SMEM, SMEM, VMEM],
+        out_shape=jax.ShapeDtypeStruct((n_dev, 2, SITE_DEV + LANES), BF16),
+        in_specs=[HBM] * 3,
         out_specs=VMEM,
-        compiler_params=params(),
-    )(ruptures, event_rupture, epsilon.reshape(2, sites))
+        scratch_shapes=[
+            pltpu.SMEM((n_rup, 6), F32),
+            pltpu.SMEM((1,), jnp.int32),
+            pltpu.VMEM((2, sites), BF16),
+            pltpu.SemaphoreType.DMA((3,)),
+        ],
+        compiler_params=params(60),
+    )(ruptures.T, event_rupture, epsilon.reshape(2, sites))
     got = exchange(packed)
 
     def as_rows(array):
         return array.reshape(asset_rows, LANES)
 
     exposure, curve = pl.pallas_call(
-        lambda *refs: exposure_kernel(t_dev, 20, *refs),
+        lambda *refs: exposure_kernel(t_dev, COMPACT_ROWS, *refs),
         out_shape=(
             jax.ShapeDtypeStruct((SITE_DEV, n_col), BF16),
             jax.ShapeDtypeStruct((t_dev, 2 * G), BF16),
         ),
-        in_specs=[VMEM] * 7,
+        in_specs=[VMEM] * 4 + [HBM] * 3,
         out_specs=(VMEM, VMEM),
         scratch_shapes=[pltpu.VMEM((asset_rows, LANES), F32)] * 4
-        + [pltpu.VMEM((SITE_DEV, n_col), F32), pltpu.VMEM((TAXO, 2 * G), F32)],
-        compiler_params=params(),
+        + [pltpu.VMEM((SITE_DEV, n_col), F32), pltpu.VMEM((TAXO, 2 * G), F32)]
+        + [pltpu.VMEM((NB, TAXO), BF16), pltpu.VMEM((1, TAXO), jnp.int32), pltpu.VMEM((1, TAXO), jnp.int32)]
+        + [pltpu.SemaphoreType.DMA((3,))],
+        compiler_params=params(24),
         cost_estimate=pl.CostEstimate(
-            flops=4 * asset_rows * LANES * SITE_DEV * n_col, bytes_accessed=1 << 20, transcendentals=0
+            flops=2 * asset_rows * LANES * SITE_DEV * n_col, bytes_accessed=1 << 20, transcendentals=0
         ),
     )(
         as_rows(asset_site),
@@ -316,10 +391,10 @@
         out_specs=VMEM,
         scratch_shapes=[
             pltpu.VMEM((n_dev, LANES), F32),
-            pltpu.VMEM((ROWS * t_dev, SITE_DEV), F32),
+            pltpu.VMEM((EVENT_BLOCK * t_dev, SITE_DEV), BF16),
             pltpu.VMEM((n_dev, n_col), F32),
         ],
-        compiler_params=params(),
+        compiler_params=params(20),
     )(got, site_coords, exposure, curve)
 
     losses = pl.pallas_call(
@@ -327,7 +402,7 @@
         out_shape=jax.ShapeDtypeStruct((n_dev // n_ev, LANES), F32),
         in_specs=[VMEM],
         out_specs=VMEM,
-        compiler_params=params(),
+        compiler_params=params(4),
     )(exchange(parts))
     return losses[None]
 

time: 35.2 us -> 29.7 us (0.84)
  Pallas kernels: 12.3 us -> 7.68 us
  blocking collectives: 11.5 us -> 9.34 us
  waiting for transfers between devices: 1.45 us -> 3.57 us
  local copies, waits for them, and re-layouts: 1.49 us -> 0.67 us
    pallas_call x1, Pallas kernels: 6.4 us -> 3.31 us  [shards(): pl.pallas_call(lambda *refs: exposure_kernel(t_dev, COMPACT_ROWS, *refs),...]
    all_to_all x1, blocking collectives: 11.5 us -> 9.34 us  [exchange(): return lax.all_to_all(array, AXES, split_axis=0, concat_axis=0, tiled=True)]
    all_to_all x1, waiting for transfers between devices: 1.45 us -> 3.57 us  [exchange(): return lax.all_to_all(array, AXES, split_axis=0, concat_axis=0, tiled=True)]
    pallas_call x1, Pallas kernels: 3.99 us -> 2.23 us  [shards(): pl.pallas_call(lambda *refs: loss_kernel(n_ev, n_site, n_rup, *refs), out...]
    unnamed x21 -> x16, local copies, waits for them, and re-layouts: 1.49 us -> 0.67 us
  transfers between devices with their start and end apart: 1 -> 1, of which waited for: 1 -> 1; matrix products, arithmetic and copies ran while one was open for 0% -> 0% of each run, Pallas kernels for 18% -> 11%
where the time goes in v2:
time: 29.7 us; the launch traced here: 29.3 us
  blocking collectives  9.34 us (31%)
  Pallas kernels  7.68 us (26%)
  starting transfers between devices  7.3 us (25%)
  waiting for transfers between devices  3.57 us (12%)
  between operations  0.77 us (3%)
  local copies, waits for them, and re-layouts  0.67 us (2%)
    all_to_all x1, blocking collectives, exchange(): return lax.all_to_all(array, AXES, split_axis=0, concat_axis=0, tiled=True)  9.34 us
    all_to_all x1, starting transfers between devices, exchange(): return lax.all_to_all(array, AXES, split_axis=0, concat_axis=0, tiled=True)  7.3 us
    all_to_all x1, waiting for transfers between devices, exchange(): return lax.all_to_all(array, AXES, split_axis=0, concat_axis=0, tiled=True)  3.57 us
    pallas_call x1, Pallas kernels, shards(): pl.pallas_call(lambda *refs: exposure_kernel(t_dev, COMPACT_ROWS, *refs),...  3.31 us
    pallas_call x1, Pallas kernels, shards(): pl.pallas_call(lambda *refs: loss_kernel(n_ev, n_site, n_rup, *refs), out...  2.23 us
    pallas_call x1, Pallas kernels, shards(): pl.pallas_call(lambda *refs: pack_kernel(n_ev, n_site, *refs), out_shape=...  1.46 us
    pallas_call x1, Pallas kernels, shards(): pl.pallas_call(lambda *refs: total_kernel(n_ev, n_site, *refs), out_shape...  0.68 us
    unnamed x16, local copies, waits for them, and re-layouts  0.67 us
  transfers between devices with their start and end apart: 1, of which 1 were waited for; matrix products, arithmetic and copies ran while one was open for 0% of the time, Pallas kernels for 11%

profile of v2, /device:TPU:0, one launch (start us, length us, event | category | flops | bytes accessed | tf_op | source)
XLA Modules:
  0.0 29.3 jit_solution(2460843431395085643)
XLA Ops:
  0.7 1.5 %shard_map.109 = bf16[32,2,640]{2,1,0:T(2,128)(2,1)} custom-call(f32[2,6]{1,0:T(2,128)} %bitcast.22, s32[1]{0:T(128)S(6)} %copy.12.refs_1_, bf16[2,4096]{1,0:T(2,128)(2,1)} %bitcast.21), custom_call_target="tpu_custom_call" | custom-call | tf_op jit(solution)/shard_map/pallas_call | solution.py:343
  2.1 0.0 copy-start.1
  2.1 0.0 copy-start.2
  2.1 0.0 copy-start.3
  2.2 0.0 copy-start.4
  2.2 7.3 %all-to-all-start = ((bf16[32,2,640]{2,1,0:T(2,128)(2,1)}), bf16[32,2,640]{2,1,0:T(2,128)(2,1)S(1)}, u32[]{:S(2)}, u32[]{:S(2)}) async-start(bf16[32,2,640]{2,1,0:T(2,128)(2,1)} %shard_map.109), calls=%async_computation | async-start | bytes 163840 | tf_op jit(solution)/shard_map/all_to_all | solution.py:341
  9.5 0.0 copy-start.5
  9.5 0.0 copy-start.6
  9.5 0.0 copy-start.7
  9.5 0.0 copy-done.1
  9.5 0.0 copy-done.2
  9.5 0.0 copy-done.3
  9.5 0.0 copy-done.4
  9.6 0.6 %copy-done.5 = bf16[128,40]{0,1:T(8,128)(2,1)S(1)} copy-done((bf16[128,40]{0,1:T(8,128)(2,1)S(1)}, bf16[128,40]{0,1:T(8,128)(2,1)}, u32[]{:S(2)}) %copy-start.5) | copy-done | bytes 10264
  10.2 0.0 copy-done.6
  10.2 0.0 copy-done.7
  10.2 0.0 copy-start
  10.2 3.3 %shard_map.110 = (bf16[512,256]{1,0:T(8,128)(2,1)S(1)}, bf16[32,128]{1,0:T(8,128)(2,1)S(1)}) custom-call(s32[80,128]{1,0:T(8,128)S(1)} %bitcast.14, s32[80,128]{1,0:T(8,128)S(1)} %bitcast.15, s32[80,128]{1,0:T(8,128)S(1)} %bitcast.16, f32[80,128]{1,0:T(8,128)S(1)} %bitcast.17, bf16[40,128]{1,0:T(8,128)(2,1)S(1)} %bitcast.18, s32[1,128]{1,0:T(1,128)S(1)} %bitcast.19, ...), custom_call_target="tpu_custom_call" | custom-call | flops 2684354560 | bytes 1048576 | tf_op jit(solution)/shard_map/pallas_call | solution.py:361
  13.5 3.6 %all-to-all-done.refs_0_ = bf16[32,2,640]{2,1,0:T(2,128)(2,1)S(1)} async-done(((bf16[32,2,640]{2,1,0:T(2,128)(2,1)}), bf16[32,2,640]{2,1,0:T(2,128)(2,1)S(1)}, u32[]{:S(2)}, u32[]{:S(2)}) %all-to-all-start) | async-done | bytes 81952 | tf_op jit(solution)/shard_map/all_to_all | solution.py:341
  17.1 0.0 copy-done
  17.1 2.2 %shard_map.111 = f32[64,128]{1,0:T(8,128)S(1)} custom-call(bf16[32,2,640]{2,1,0:T(2,128)(2,1)S(1)} %all-to-all-done.refs_0_, f32[2,4096]{1,0:T(2,128)S(1)} %copy-done, bf16[512,256]{1,0:T(8,128)(2,1)S(1)} %get-tuple-element.7.refs_2_, bf16[32,128]{1,0:T(8,128)(2,1)S(1)} %get-tuple-element.8.refs_3_), custom_call_target="tpu_custom_call" | custom-call | tf_op jit(solution)/shard_map/pallas_call | solution.py:387
  19.3 9.3 %all_to_all.16 = f32[32,2,128]{2,1,0:T(2,128)S(1)} all-to-all(f32[32,2,128]{2,1,0:T(2,128)S(1)} %bitcast.12), channel_id=1, replica_groups=mesh['ev'=4,'site'=8] {'ev','site'}, dimensions={0} | all-to-all | bytes 65536 | tf_op jit(solution)/shard_map/all_to_all | solution.py:341
  28.7 0.7 %shard_map.112 = f32[8,128]{1,0:T(8,128)} custom-call(f32[64,128]{1,0:T(8,128)S(1)} %bitcast.13), custom_call_target="tpu_custom_call" | custom-call | tf_op jit(solution)/shard_map/pallas_call | solution.py:400
Async XLA Ops:
  2.1 7.4 %copy-start.1 = (s32[10240]{0:T(1024)S(1)}, s32[10240]{0:T(1024)}, u32[]{:S(2)}) copy-start(s32[10240]{0:T(1024)} %param.18) | copy-start | bytes 122884
  2.1 7.4 %copy-start.2 = (s32[10240]{0:T(1024)S(1)}, s32[10240]{0:T(1024)}, u32[]{:S(2)}) copy-start(s32[10240]{0:T(1024)} %param.19) | copy-start | bytes 122884
  2.1 7.4 %copy-start.3 = (s32[10240]{0:T(1024)S(1)}, s32[10240]{0:T(1024)}, u32[]{:S(2)}) copy-start(s32[10240]{0:T(1024)} %param.20) | copy-start | bytes 122884
  2.2 7.4 %copy-start.4 = (f32[10240]{0:T(1024)S(1)}, f32[10240]{0:T(1024)}, u32[]{:S(2)}) copy-start(f32[10240]{0:T(1024)} %param.21) | copy-start | bytes 122884
  2.2 14.9 %all-to-all-start = ((bf16[32,2,640]{2,1,0:T(2,128)(2,1)}), bf16[32,2,640]{2,1,0:T(2,128)(2,1)S(1)}, u32[]{:S(2)}, u32[]{:S(2)}) async-start(bf16[32,2,640]{2,1,0:T(2,128)(2,1)} %shard_map.109), calls=%async_computation | async-start | bytes 163840 | tf_op jit(solution)/shard_map/all_to_all | solution.py:341
  9.5 0.7 %copy-start.5 = (bf16[128,40]{0,1:T(8,128)(2,1)S(1)}, bf16[128,40]{0,1:T(8,128)(2,1)}, u32[]{:S(2)}) copy-start(bf16[128,40]{0,1:T(8,128)(2,1)} %param.15) | copy-start | bytes 30724
  9.5 0.7 %copy-start.6 = (s32[128]{0:T(128)S(1)}, s32[128]{0:T(128)}, u32[]{:S(2)}) copy-start(s32[128]{0:T(128)} %param.16) | copy-start | bytes 1540
  9.5 0.7 %copy-start.7 = (s32[128]{0:T(128)S(1)}, s32[128]{0:T(128)}, u32[]{:S(2)}) copy-start(s32[128]{0:T(128)} %param.17) | copy-start | bytes 1540
  10.2 6.9 %copy-start = (f32[2,4096]{1,0:T(2,128)S(1)}, f32[2,4096]{1,0:T(2,128)}, u32[]{:S(2)}) copy-start(f32[2,4096]{1,0:T(2,128)} %refs_1_.2) | copy-start | bytes 98308

commit v3 on v2

--- a/solution.py
+++ b/solution.py
@@ -337,12 +337,15 @@
     n_col = n_site * t_dev
     asset_rows = asset_site.shape[0] // LANES
 
+    def stays(array):
+        return pltpu.with_memory_space_constraint(array, pltpu.HBM)
+
     def exchange(array):
         return lax.all_to_all(array, AXES, split_axis=0, concat_axis=0, tiled=True)
 
     packed = pl.pallas_call(
         lambda *refs: pack_kernel(n_ev, n_site, *refs),
-        out_shape=jax.ShapeDtypeStruct((n_dev, 2, SITE_DEV + LANES), BF16),
+        out_shape=pltpu.VMEM((n_dev, 2, SITE_DEV + LANES), BF16),
         in_specs=[HBM] * 3,
         out_specs=VMEM,
         scratch_shapes=[
@@ -351,8 +354,8 @@
             pltpu.VMEM((2, sites), BF16),
             pltpu.SemaphoreType.DMA((3,)),
         ],
-        compiler_params=params(60),
-    )(ruptures.T, event_rupture, epsilon.reshape(2, sites))
+        compiler_params=params(4),
+    )(stays(ruptures.T), event_rupture, stays(epsilon.reshape(2, sites)))
     got = exchange(packed)
 
     def as_rows(array):
@@ -379,9 +382,9 @@
         as_rows(asset_taxo),
         as_rows(asset_tract),
         as_rows(asset_value),
-        vulnerability.T,
-        taxo_measure.reshape(1, TAXO),
-        taxo_offset.reshape(1, TAXO),
+        stays(vulnerability.T),
+        stays(taxo_measure.reshape(1, TAXO)),
+        stays(taxo_offset.reshape(1, TAXO)),
     )
 
     parts = pl.pallas_call(

time: 29.7 us -> 29.2 us (0.983)
  waiting for transfers between devices: 3.57 us -> 4.23 us
  local copies, waits for them, and re-layouts: 0.67 us -> 0.03 us
  blocking collectives: 9.34 us -> 8.93 us
    all_to_all x1, waiting for transfers between devices: 3.57 us -> 4.23 us  [exchange(): return lax.all_to_all(array, AXES, split_axis=0, concat_axis=0, tiled=True)]
    unnamed x16 -> x10, local copies, waits for them, and re-layouts: 0.67 us -> 0.03 us
    all_to_all x1, blocking collectives: 9.34 us -> 8.93 us  [exchange(): return lax.all_to_all(array, AXES, split_axis=0, concat_axis=0, tiled=True)]
where the time goes in v3:
time: 29.2 us; the launch traced here: 28.9 us
  blocking collectives  8.93 us (31%)
  Pallas kernels  7.68 us (26%)
  starting transfers between devices  7.3 us (25%)
  waiting for transfers between devices  4.23 us (14%)
  between operations  0.75 us (3%)
    all_to_all x1, blocking collectives, exchange(): return lax.all_to_all(array, AXES, split_axis=0, concat_axis=0, tiled=True)  8.93 us
    all_to_all x1, starting transfers between devices, exchange(): return lax.all_to_all(array, AXES, split_axis=0, concat_axis=0, tiled=True)  7.3 us
    all_to_all x1, waiting for transfers between devices, exchange(): return lax.all_to_all(array, AXES, split_axis=0, concat_axis=0, tiled=True)  4.23 us
    pallas_call x1, Pallas kernels, shards(): pl.pallas_call(lambda *refs: exposure_kernel(t_dev, COMPACT_ROWS, *refs),...  3.31 us
    pallas_call x1, Pallas kernels, shards(): pl.pallas_call(lambda *refs: loss_kernel(n_ev, n_site, n_rup, *refs), out...  2.23 us
    pallas_call x1, Pallas kernels, shards(): pl.pallas_call(lambda *refs: pack_kernel(n_ev, n_site, *refs), out_shape=...  1.46 us
    pallas_call x1, Pallas kernels, shards(): pl.pallas_call(lambda *refs: total_kernel(n_ev, n_site, *refs), out_shape...  0.68 us
  transfers between devices with their start and end apart: 1, of which 1 were waited for; matrix products, arithmetic and copies ran while one was open for 0% of the time, Pallas kernels for 11%

profile of v3, /device:TPU:0, one launch (start us, length us, event | category | flops | bytes accessed | tf_op | source)
XLA Modules:
  0.0 28.9 jit_solution(11767243985034562863)
XLA Ops:
  0.7 1.5 %shard_map.109 = bf16[32,2,640]{2,1,0:T(2,128)(2,1)} custom-call(f32[2,6]{1,0:T(2,128)} %bitcast.19, s32[1]{0:T(128)S(6)} %copy.12.refs_1_, bf16[2,4096]{1,0:T(2,128)(2,1)} %bitcast.18), custom_call_target="tpu_custom_call" | custom-call | tf_op jit(solution)/shard_map/pallas_call | solution.py:346
  2.1 0.0 copy-start.1
  2.1 0.0 copy-start.2
  2.1 0.0 copy-start.3
  2.2 0.0 copy-start.4
  2.2 7.3 %all-to-all-start = ((bf16[32,2,640]{2,1,0:T(2,128)(2,1)}), bf16[32,2,640]{2,1,0:T(2,128)(2,1)S(1)}, u32[]{:S(2)}, u32[]{:S(2)}) async-start(bf16[32,2,640]{2,1,0:T(2,128)(2,1)} %shard_map.109), calls=%async_computation | async-start | bytes 163840 | tf_op jit(solution)/shard_map/all_to_all | solution.py:344
  9.5 0.0 copy-done.1
  9.5 0.0 copy-done.2
  9.5 0.0 copy-done.3
  9.5 0.0 copy-done.4
  9.5 0.0 copy-start
  9.5 3.3 %shard_map.110 = (bf16[512,256]{1,0:T(8,128)(2,1)S(1)}, bf16[32,128]{1,0:T(8,128)(2,1)S(1)}) custom-call(s32[80,128]{1,0:T(8,128)S(1)} %bitcast.14, s32[80,128]{1,0:T(8,128)S(1)} %bitcast.15, s32[80,128]{1,0:T(8,128)S(1)} %bitcast.16, f32[80,128]{1,0:T(8,128)S(1)} %bitcast.17, bf16[40,128]{1,0:T(8,128)(2,1)} %bitcast.20, s32[1,128]{1,0:T(1,128)} %bitcast.21, ...), custom_call_target="tpu_custom_call" | custom-call | flops 2684354560 | bytes 1048576 | tf_op jit(solution)/shard_map/pallas_call | solution.py:364
  12.9 4.2 %all-to-all-done.refs_0_ = bf16[32,2,640]{2,1,0:T(2,128)(2,1)S(1)} async-done(((bf16[32,2,640]{2,1,0:T(2,128)(2,1)}), bf16[32,2,640]{2,1,0:T(2,128)(2,1)S(1)}, u32[]{:S(2)}, u32[]{:S(2)}) %all-to-all-start) | async-done | bytes 81952 | tf_op jit(solution)/shard_map/all_to_all | solution.py:344
  17.1 0.0 copy-done
  17.1 2.2 %shard_map.111 = f32[64,128]{1,0:T(8,128)S(1)} custom-call(bf16[32,2,640]{2,1,0:T(2,128)(2,1)S(1)} %all-to-all-done.refs_0_, f32[2,4096]{1,0:T(2,128)S(1)} %copy-done, bf16[512,256]{1,0:T(8,128)(2,1)S(1)} %get-tuple-element.7.refs_2_, bf16[32,128]{1,0:T(8,128)(2,1)S(1)} %get-tuple-element.8.refs_3_), custom_call_target="tpu_custom_call" | custom-call | tf_op jit(solution)/shard_map/pallas_call | solution.py:390
  19.3 8.9 %all_to_all.16 = f32[32,2,128]{2,1,0:T(2,128)S(1)} all-to-all(f32[32,2,128]{2,1,0:T(2,128)S(1)} %bitcast.12), channel_id=1, replica_groups=mesh['ev'=4,'site'=8] {'ev','site'}, dimensions={0} | all-to-all | bytes 65536 | tf_op jit(solution)/shard_map/all_to_all | solution.py:344
  28.3 0.7 %shard_map.112 = f32[8,128]{1,0:T(8,128)} custom-call(f32[64,128]{1,0:T(8,128)S(1)} %bitcast.13), custom_call_target="tpu_custom_call" | custom-call | tf_op jit(solution)/shard_map/pallas_call | solution.py:403
Async XLA Ops:
  2.1 7.4 %copy-start.1 = (s32[10240]{0:T(1024)S(1)}, s32[10240]{0:T(1024)}, u32[]{:S(2)}) copy-start(s32[10240]{0:T(1024)} %param.18) | copy-start | bytes 122884
  2.1 7.4 %copy-start.2 = (s32[10240]{0:T(1024)S(1)}, s32[10240]{0:T(1024)}, u32[]{:S(2)}) copy-start(s32[10240]{0:T(1024)} %param.19) | copy-start | bytes 122884
  2.1 7.4 %copy-start.3 = (s32[10240]{0:T(1024)S(1)}, s32[10240]{0:T(1024)}, u32[]{:S(2)}) copy-start(s32[10240]{0:T(1024)} %param.20) | copy-start | bytes 122884
  2.2 7.4 %copy-start.4 = (f32[10240]{0:T(1024)S(1)}, f32[10240]{0:T(1024)}, u32[]{:S(2)}) copy-start(f32[10240]{0:T(1024)} %param.21) | copy-start | bytes 122884
  2.2 14.9 %all-to-all-start = ((bf16[32,2,640]{2,1,0:T(2,128)(2,1)}), bf16[32,2,640]{2,1,0:T(2,128)(2,1)S(1)}, u32[]{:S(2)}, u32[]{:S(2)}) async-start(bf16[32,2,640]{2,1,0:T(2,128)(2,1)} %shard_map.109), calls=%async_computation | async-start | bytes 163840 | tf_op jit(solution)/shard_map/all_to_all | solution.py:344
  9.5 7.6 %copy-start = (f32[2,4096]{1,0:T(2,128)S(1)}, f32[2,4096]{1,0:T(2,128)}, u32[]{:S(2)}) copy-start(f32[2,4096]{1,0:T(2,128)} %refs_1_.2) | copy-start | bytes 98308

commit v4 on v3

--- a/solution.py
+++ b/solution.py
@@ -28,6 +28,7 @@
 NT = (((1,), (1,)), ((), ()))
 
 VMEM = pl.BlockSpec(memory_space=pltpu.VMEM)
+SMEM = pl.BlockSpec(memory_space=pltpu.SMEM)
 HBM = pl.BlockSpec(memory_space=pltpu.HBM)
 
 
@@ -42,25 +43,23 @@
     return high, middle, (rest - middle).astype(BF16).astype(F32)
 
 
-def pack_kernel(n_ev, n_site, rup_hbm, idx_hbm, eps_hbm, out_ref, rup_ref, idx_ref, eps_ref, sems):
-    copies = [
-        pltpu.make_async_copy(source, target, sems.at[k])
-        for k, (source, target) in enumerate(((rup_hbm, rup_ref), (idx_hbm, idx_ref), (eps_hbm, eps_ref)))
-    ]
-    for copy in copies:
-        copy.start()
-    n_rup = rup_ref.shape[0]
-    lane = lax.broadcasted_iota(jnp.int32, (2, LANES), 1)
-    row = jnp.zeros((2, LANES), F32)
-    copies[0].wait()
-    copies[1].wait()
-    for b in range(n_rup):
-        for c in range(6):
-            row = jnp.where(lane == 6 * b + c, rup_ref[b, c], row)
+def place_kernel(out_ref):
+    out_ref[...] = lax.broadcasted_iota(jnp.int32, out_ref.shape, 1) - lax.broadcasted_iota(
+        jnp.int32, out_ref.shape, 0
+    )
+
+
+def pack_kernel(n_ev, n_site, place_ref, rup_ref, idx_ref, eps_ref, out_ref):
+    n_rup = rup_ref.shape[1]
+    place = place_ref[0:6, :]
+    spots = jnp.zeros((6, LANES), F32)
+    for k in range(n_rup):
+        spots = jnp.where(place == 6 * k, jnp.broadcast_to(rup_ref[:, k : k + 1], (6, LANES)), spots)
+    row = jnp.broadcast_to(jnp.sum(spots, axis=0, keepdims=True), (2, LANES))
+    lane = jnp.broadcast_to(place_ref[0:1, :], (2, LANES))
     row = jnp.where(lane == 6 * n_rup, idx_ref[0].astype(F32), row)
     high, middle, low = parts_of(row)
     row = (high + pltpu.roll(middle, PART, 1) + pltpu.roll(low, 2 * PART, 1)).astype(BF16)
-    copies[2].wait()
     eps = eps_ref[...]
 
     def fill(i, carry):
@@ -343,19 +342,20 @@
     def exchange(array):
         return lax.all_to_all(array, AXES, split_axis=0, concat_axis=0, tiled=True)
 
+    place = pl.pallas_call(
+        place_kernel,
+        out_shape=jax.ShapeDtypeStruct((ROWS, LANES), jnp.int32),
+        out_specs=VMEM,
+        compiler_params=params(4),
+        cost_estimate=pl.CostEstimate(flops=4_000_000_000, bytes_accessed=12_000_000, transcendentals=0),
+    )()
     packed = pl.pallas_call(
         lambda *refs: pack_kernel(n_ev, n_site, *refs),
-        out_shape=pltpu.VMEM((n_dev, 2, SITE_DEV + LANES), BF16),
-        in_specs=[HBM] * 3,
+        out_shape=jax.ShapeDtypeStruct((n_dev, 2, SITE_DEV + LANES), BF16),
+        in_specs=[VMEM, VMEM, SMEM, VMEM],
         out_specs=VMEM,
-        scratch_shapes=[
-            pltpu.SMEM((n_rup, 6), F32),
-            pltpu.SMEM((1,), jnp.int32),
-            pltpu.VMEM((2, sites), BF16),
-            pltpu.SemaphoreType.DMA((3,)),
-        ],
         compiler_params=params(4),
-    )(stays(ruptures.T), event_rupture, stays(epsilon.reshape(2, sites)))
+    )(place, ruptures, event_rupture, epsilon.reshape(2, sites))
     got = exchange(packed)
 
     def as_rows(array):

time: 29.2 us -> 28.6 us (0.979)
  Pallas kernels: 7.68 us -> 7.03 us
    pallas_call x1, Pallas kernels: 1.46 us -> 0.79 us  [shards(): pl.pallas_call(lambda *refs: pack_kernel(n_ev, n_site, *refs), out_shape=...]
  transfers between devices with their start and end apart: 1 -> 1, of which waited for: 1 -> 1; matrix products, arithmetic and copies ran while one was open for 0% -> 0% of each run, Pallas kernels for 11% -> 12%
where the time goes in v4:
time: 28.6 us; the launch traced here: 28.4 us
  blocking collectives  8.93 us (31%)
  starting transfers between devices  7.3 us (26%)
  Pallas kernels  7.03 us (25%)
  waiting for transfers between devices  4.23 us (15%)
  between operations  0.74 us (3%)
    all_to_all x1, blocking collectives, exchange(): return lax.all_to_all(array, AXES, split_axis=0, concat_axis=0, tiled=True)  8.93 us
    all_to_all x1, starting transfers between devices, exchange(): return lax.all_to_all(array, AXES, split_axis=0, concat_axis=0, tiled=True)  7.3 us
    all_to_all x1, waiting for transfers between devices, exchange(): return lax.all_to_all(array, AXES, split_axis=0, concat_axis=0, tiled=True)  4.23 us
    pallas_call x1, Pallas kernels, shards(): pl.pallas_call(lambda *refs: exposure_kernel(t_dev, COMPACT_ROWS, *refs),...  3.32 us
    pallas_call x1, Pallas kernels, shards(): pl.pallas_call(lambda *refs: loss_kernel(n_ev, n_site, n_rup, *refs), out...  2.24 us
    pallas_call x1, Pallas kernels, shards(): pl.pallas_call(lambda *refs: pack_kernel(n_ev, n_site, *refs), out_shape=...  0.79 us
    pallas_call x1, Pallas kernels, shards(): pl.pallas_call(lambda *refs: total_kernel(n_ev, n_site, *refs), out_shape...  0.68 us
  transfers between devices with their start and end apart: 1, of which 1 were waited for; matrix products, arithmetic and copies ran while one was open for 0% of the time, Pallas kernels for 12%

profile of v4, /device:TPU:0, one launch (start us, length us, event | category | flops | bytes accessed | tf_op | source)
XLA Modules:
  0.0 28.4 jit_solution(18441324663476289269)
XLA Ops:
  0.0 0.0 copy-start.1
  0.0 0.0 copy-start.6
  0.7 0.0 copy-done.6
  0.7 0.1 copy.12.refs_1_
  0.8 0.0 copy-done.1
  0.8 0.8 %shard_map.110 = bf16[32,2,640]{2,1,0:T(2,128)(2,1)} custom-call(s32[8,128]{1,0:T(8,128)S(1)} %shard_map.109.refs_0_, f32[6,2]{1,0:T(8,128)S(1)} %copy.12.refs_1_, s32[1]{0:T(128)S(6)} %copy.13.refs_2_, bf16[2,4096]{1,0:T(2,128)(2,1)S(1)} %bitcast.13), custom_call_target="tpu_custom_call" | custom-call | tf_op jit(solution)/shard_map/pallas_call | solution.py:352
  1.6 0.0 copy-start.2
  1.6 0.0 copy-start.3
  1.6 0.0 copy-start.4
  1.6 0.0 copy-start.5
  1.6 7.3 %all-to-all-start = ((bf16[32,2,640]{2,1,0:T(2,128)(2,1)}), bf16[32,2,640]{2,1,0:T(2,128)(2,1)S(1)}, u32[]{:S(2)}, u32[]{:S(2)}) async-start(bf16[32,2,640]{2,1,0:T(2,128)(2,1)} %shard_map.110), calls=%async_computation | async-start | bytes 163840 | tf_op jit(solution)/shard_map/all_to_all | solution.py:343
  8.9 0.0 copy-done.2
  8.9 0.0 copy-done.3
  8.9 0.0 copy-done.4
  8.9 0.0 copy-done.5
  8.9 0.0 copy-start
  9.0 3.3 %shard_map.111 = (bf16[512,256]{1,0:T(8,128)(2,1)S(1)}, bf16[32,128]{1,0:T(8,128)(2,1)S(1)}) custom-call(s32[80,128]{1,0:T(8,128)S(1)} %bitcast.14, s32[80,128]{1,0:T(8,128)S(1)} %bitcast.15, s32[80,128]{1,0:T(8,128)S(1)} %bitcast.16, f32[80,128]{1,0:T(8,128)S(1)} %bitcast.17, bf16[40,128]{1,0:T(8,128)(2,1)} %bitcast.18, s32[1,128]{1,0:T(1,128)} %bitcast.19, ...), custom_call_target="tpu_custom_call" | custom-call | flops 2684354560 | bytes 1048576 | tf_op jit(solution)/shard_map/pallas_call | solution.py:364
  12.3 4.2 %all-to-all-done.refs_0_ = bf16[32,2,640]{2,1,0:T(2,128)(2,1)S(1)} async-done(((bf16[32,2,640]{2,1,0:T(2,128)(2,1)}), bf16[32,2,640]{2,1,0:T(2,128)(2,1)S(1)}, u32[]{:S(2)}, u32[]{:S(2)}) %all-to-all-start) | async-done | bytes 81952 | tf_op jit(solution)/shard_map/all_to_all | solution.py:343
  16.5 0.0 copy-done
  16.5 2.2 %shard_map.112 = f32[64,128]{1,0:T(8,128)S(1)} custom-call(bf16[32,2,640]{2,1,0:T(2,128)(2,1)S(1)} %all-to-all-done.refs_0_, f32[2,4096]{1,0:T(2,128)S(1)} %copy-done, bf16[512,256]{1,0:T(8,128)(2,1)S(1)} %get-tuple-element.7.refs_2_, bf16[32,128]{1,0:T(8,128)(2,1)S(1)} %get-tuple-element.8.refs_3_), custom_call_target="tpu_custom_call" | custom-call | tf_op jit(solution)/shard_map/pallas_call | solution.py:390
  18.7 8.9 %all_to_all.16 = f32[32,2,128]{2,1,0:T(2,128)S(1)} all-to-all(f32[32,2,128]{2,1,0:T(2,128)S(1)} %bitcast.11), channel_id=1, replica_groups=mesh['ev'=4,'site'=8] {'ev','site'}, dimensions={0} | all-to-all | bytes 65536 | tf_op jit(solution)/shard_map/all_to_all | solution.py:343
  27.7 0.7 %shard_map.113 = f32[8,128]{1,0:T(8,128)} custom-call(f32[64,128]{1,0:T(8,128)S(1)} %bitcast.12), custom_call_target="tpu_custom_call" | custom-call | tf_op jit(solution)/shard_map/pallas_call | solution.py:403
  (1 shorter events, 0.0 us)
Async XLA Ops:
  0.0 0.8 %copy-start.1 = (bf16[2,1,4096]{2,0,1:T(2,128)(2,1)S(1)}, bf16[2,1,4096]{2,0,1:T(2,128)(2,1)}, u32[]{:S(2)}) copy-start(bf16[2,1,4096]{2,0,1:T(2,128)(2,1)} %param.13) | copy-start | bytes 49156
  0.0 0.7 %copy-start.6 = (f32[6,2]{0,1:T(2,128)S(1)}, f32[6,2]{0,1:T(2,128)}, u32[]{:S(2)}) copy-start(f32[6,2]{0,1:T(2,128)} %param.11) | copy-start | bytes 148
  1.6 7.3 %copy-start.2 = (s32[10240]{0:T(1024)S(1)}, s32[10240]{0:T(1024)}, u32[]{:S(2)}) copy-start(s32[10240]{0:T(1024)} %param.18) | copy-start | bytes 122884
  1.6 7.3 %copy-start.3 = (s32[10240]{0:T(1024)S(1)}, s32[10240]{0:T(1024)}, u32[]{:S(2)}) copy-start(s32[10240]{0:T(1024)} %param.19) | copy-start | bytes 122884
  1.6 7.3 %copy-start.4 = (s32[10240]{0:T(1024)S(1)}, s32[10240]{0:T(1024)}, u32[]{:S(2)}) copy-start(s32[10240]{0:T(1024)} %param.20) | copy-start | bytes 122884
  1.6 7.3 %copy-start.5 = (f32[10240]{0:T(1024)S(1)}, f32[10240]{0:T(1024)}, u32[]{:S(2)}) copy-start(f32[10240]{0:T(1024)} %param.21) | copy-start | bytes 122884
  1.6 14.9 %all-to-all-start = ((bf16[32,2,640]{2,1,0:T(2,128)(2,1)}), bf16[32,2,640]{2,1,0:T(2,128)(2,1)S(1)}, u32[]{:S(2)}, u32[]{:S(2)}) async-start(bf16[32,2,640]{2,1,0:T(2,128)(2,1)} %shard_map.110), calls=%async_computation | async-start | bytes 163840 | tf_op jit(solution)/shard_map/all_to_all | solution.py:343
  8.9 7.6 %copy-start = (f32[2,4096]{1,0:T(2,128)S(1)}, f32[2,4096]{1,0:T(2,128)}, u32[]{:S(2)}) copy-start(f32[2,4096]{1,0:T(2,128)} %refs_1_.2) | copy-start | bytes 98308

commit v5 on v4

--- a/solution.py
+++ b/solution.py
@@ -200,14 +200,16 @@
     x = coords_ref[0:1, pl.ds(start, SITE_DEV)]
     y = coords_ref[1:2, pl.ds(start, SITE_DEV)]
 
-    def take_geometry(b, carry):
-        first = b * EVENT_BLOCK
-        rows = [got_ref[first + u, :, SITE_DEV:].astype(F32)[0:1] for u in range(EVENT_BLOCK)]
-        geo_s[pl.ds(pl.multiple_of(first, ROWS), EVENT_BLOCK), :] = jnp.concatenate(rows, axis=0)
-        return carry
-
-    lax.fori_loop(0, n_dev // EVENT_BLOCK, take_geometry, 0)
-    ruptures = geo_s[...].astype(BF16)
+    every = got_ref[:, :, SITE_DEV:].astype(F32)[:, 0, :]
+    geo_s[...] = every
+    table = jnp.concatenate(
+        [
+            every if u == 0 and p == 0 else pltpu.roll(every, LANES - 6 * u - PART * p, 1)
+            for p in range(3)
+            for u in range(n_rup)
+        ],
+        axis=0,
+    ).astype(BF16)
     level = lax.broadcasted_iota(jnp.int32, (G, SITE_DEV), 0).astype(F32).astype(BF16)
     level_less = (lax.broadcasted_iota(jnp.int32, (G, SITE_DEV), 0) - 1).astype(F32).astype(BF16)
     zero = jnp.zeros((G, SITE_DEV), BF16)
@@ -224,12 +226,9 @@
         first = pl.multiple_of(b * EVENT_BLOCK, EVENT_BLOCK)
         here = joined(geo_s[pl.ds(first, EVENT_BLOCK), :])
         rupture = here[:, 6 * n_rup : 6 * n_rup + 1].astype(jnp.int32)
-        owner = rupture // n_rup
-        hot = (lax.broadcasted_iota(jnp.int32, (EVENT_BLOCK, n_dev), 1) == owner).astype(BF16)
-        found = joined(jnp.dot(hot, ruptures, preferred_element_type=F32))
-        own = found
-        for u in range(1, n_rup):
-            own = jnp.where(rupture - owner * n_rup == u, pltpu.roll(found, LANES - 6 * u, 1), own)
+        place = lax.broadcasted_iota(jnp.int32, (EVENT_BLOCK, n_dev), 1) * n_rup
+        hot = jnp.concatenate([(place + u == rupture).astype(BF16) for u in range(n_rup)] * 3, axis=1)
+        own = jnp.dot(hot, table, preferred_element_type=F32)
         start_x = own[:, 0:1]
         start_y = own[:, 1:2]
         along_x = own[:, 2:3] - start_x
@@ -243,11 +242,11 @@
         off_x = rel_x - portion * along_x
         off_y = rel_y - portion * along_y
         distance = jnp.sqrt(off_x * off_x + off_y * off_y + depth * depth)
-        got = [got_ref[b * EVENT_BLOCK + u, :, :SITE_DEV].astype(F32) for u in range(EVENT_BLOCK)]
+        got = got_ref[pl.ds(b * EVENT_BLOCK, EVENT_BLOCK), :, :SITE_DEV].astype(F32)
         below, weight_0, weight_1 = [], [], []
         for k in range(2):
             c = COEFFS[k]
-            eps = jnp.concatenate([rows[k : k + 1] for rows in got], axis=0)
+            eps = got[:, k, :]
             field = (
                 c[0] + c[1] * (size - 6.0)
                 - c[2] * 0.5 * jnp.log(distance * distance + c[3] * c[3])

time: 28.6 us -> 28.5 us (level)
  no operation moved by 1% of the time
where the time goes in v5:
time: 28.5 us; the launch traced here: 28.2 us
  blocking collectives  8.95 us (31%)
  starting transfers between devices  7.3 us (26%)
  Pallas kernels  6.88 us (24%)
  waiting for transfers between devices  4.23 us (15%)
  between operations  0.75 us (3%)
    all_to_all x1, blocking collectives, exchange(): return lax.all_to_all(array, AXES, split_axis=0, concat_axis=0, tiled=True)  8.95 us
    all_to_all x1, starting transfers between devices, exchange(): return lax.all_to_all(array, AXES, split_axis=0, concat_axis=0, tiled=True)  7.3 us
    all_to_all x1, waiting for transfers between devices, exchange(): return lax.all_to_all(array, AXES, split_axis=0, concat_axis=0, tiled=True)  4.23 us
    pallas_call x1, Pallas kernels, shards(): pl.pallas_call(lambda *refs: exposure_kernel(t_dev, COMPACT_ROWS, *refs),...  3.32 us
    pallas_call x1, Pallas kernels, shards(): pl.pallas_call(lambda *refs: loss_kernel(n_ev, n_site, n_rup, *refs), out...  2.09 us
    pallas_call x1, Pallas kernels, shards(): pl.pallas_call(lambda *refs: pack_kernel(n_ev, n_site, *refs), out_shape=...  0.79 us
    pallas_call x1, Pallas kernels, shards(): pl.pallas_call(lambda *refs: total_kernel(n_ev, n_site, *refs), out_shape...  0.68 us
  transfers between devices with their start and end apart: 1, of which 1 were waited for; matrix products, arithmetic and copies ran while one was open for 0% of the time, Pallas kernels for 12%

profile of v5, /device:TPU:0, one launch (start us, length us, event | category | flops | bytes accessed | tf_op | source)
XLA Modules:
  0.0 28.2 jit_solution(5247894595679135803)
XLA Ops:
  0.0 0.0 copy-start.1
  0.0 0.0 copy-start.6
  0.7 0.0 copy-done.6
  0.7 0.1 copy.12.refs_1_
  0.8 0.0 copy-done.1
  0.8 0.8 %shard_map.110 = bf16[32,2,640]{2,1,0:T(2,128)(2,1)} custom-call(s32[8,128]{1,0:T(8,128)S(1)} %shard_map.109.refs_0_, f32[6,2]{1,0:T(8,128)S(1)} %copy.12.refs_1_, s32[1]{0:T(128)S(6)} %copy.13.refs_2_, bf16[2,4096]{1,0:T(2,128)(2,1)S(1)} %bitcast.13), custom_call_target="tpu_custom_call" | custom-call | tf_op jit(solution)/shard_map/pallas_call | solution.py:351
  1.6 0.0 copy-start.2
  1.6 0.0 copy-start.3
  1.6 0.0 copy-start.4
  1.6 0.0 copy-start.5
  1.6 7.3 %all-to-all-start = ((bf16[32,2,640]{2,1,0:T(2,128)(2,1)}), bf16[32,2,640]{2,1,0:T(2,128)(2,1)S(1)}, u32[]{:S(2)}, u32[]{:S(2)}) async-start(bf16[32,2,640]{2,1,0:T(2,128)(2,1)} %shard_map.110), calls=%async_computation | async-start | bytes 163840 | tf_op jit(solution)/shard_map/all_to_all | solution.py:342
  8.9 0.0 copy-done.2
  8.9 0.0 copy-done.3
  8.9 0.0 copy-done.4
  8.9 0.0 copy-done.5
  8.9 0.0 copy-start
  9.0 3.3 %shard_map.111 = (bf16[512,256]{1,0:T(8,128)(2,1)S(1)}, bf16[32,128]{1,0:T(8,128)(2,1)S(1)}) custom-call(s32[80,128]{1,0:T(8,128)S(1)} %bitcast.14, s32[80,128]{1,0:T(8,128)S(1)} %bitcast.15, s32[80,128]{1,0:T(8,128)S(1)} %bitcast.16, f32[80,128]{1,0:T(8,128)S(1)} %bitcast.17, bf16[40,128]{1,0:T(8,128)(2,1)} %bitcast.18, s32[1,128]{1,0:T(1,128)} %bitcast.19, ...), custom_call_target="tpu_custom_call" | custom-call | flops 2684354560 | bytes 1048576 | tf_op jit(solution)/shard_map/pallas_call | solution.py:363
  12.3 4.2 %all-to-all-done.refs_0_ = bf16[32,2,640]{2,1,0:T(2,128)(2,1)S(1)} async-done(((bf16[32,2,640]{2,1,0:T(2,128)(2,1)}), bf16[32,2,640]{2,1,0:T(2,128)(2,1)S(1)}, u32[]{:S(2)}, u32[]{:S(2)}) %all-to-all-start) | async-done | bytes 81952 | tf_op jit(solution)/shard_map/all_to_all | solution.py:342
  16.5 0.0 copy-done
  16.5 2.1 %shard_map.112 = f32[64,128]{1,0:T(8,128)S(1)} custom-call(bf16[32,2,640]{2,1,0:T(2,128)(2,1)S(1)} %all-to-all-done.refs_0_, f32[2,4096]{1,0:T(2,128)S(1)} %copy-done, bf16[512,256]{1,0:T(8,128)(2,1)S(1)} %get-tuple-element.7.refs_2_, bf16[32,128]{1,0:T(8,128)(2,1)S(1)} %get-tuple-element.8.refs_3_), custom_call_target="tpu_custom_call" | custom-call | tf_op jit(solution)/shard_map/pallas_call | solution.py:389
  18.6 8.9 %all_to_all.16 = f32[32,2,128]{2,1,0:T(2,128)S(1)} all-to-all(f32[32,2,128]{2,1,0:T(2,128)S(1)} %bitcast.11), channel_id=1, replica_groups=mesh['ev'=4,'site'=8] {'ev','site'}, dimensions={0} | all-to-all | bytes 65536 | tf_op jit(solution)/shard_map/all_to_all | solution.py:342
  27.6 0.7 %shard_map.113 = f32[8,128]{1,0:T(8,128)} custom-call(f32[64,128]{1,0:T(8,128)S(1)} %bitcast.12), custom_call_target="tpu_custom_call" | custom-call | tf_op jit(solution)/shard_map/pallas_call | solution.py:402
  (1 shorter events, 0.0 us)
Async XLA Ops:
  0.0 0.8 %copy-start.1 = (bf16[2,1,4096]{2,0,1:T(2,128)(2,1)S(1)}, bf16[2,1,4096]{2,0,1:T(2,128)(2,1)}, u32[]{:S(2)}) copy-start(bf16[2,1,4096]{2,0,1:T(2,128)(2,1)} %param.13) | copy-start | bytes 49156
  0.0 0.7 %copy-start.6 = (f32[6,2]{0,1:T(2,128)S(1)}, f32[6,2]{0,1:T(2,128)}, u32[]{:S(2)}) copy-start(f32[6,2]{0,1:T(2,128)} %param.11) | copy-start | bytes 148
  1.6 7.3 %copy-start.2 = (s32[10240]{0:T(1024)S(1)}, s32[10240]{0:T(1024)}, u32[]{:S(2)}) copy-start(s32[10240]{0:T(1024)} %param.18) | copy-start | bytes 122884
  1.6 7.3 %copy-start.3 = (s32[10240]{0:T(1024)S(1)}, s32[10240]{0:T(1024)}, u32[]{:S(2)}) copy-start(s32[10240]{0:T(1024)} %param.19) | copy-start | bytes 122884
  1.6 7.3 %copy-start.4 = (s32[10240]{0:T(1024)S(1)}, s32[10240]{0:T(1024)}, u32[]{:S(2)}) copy-start(s32[10240]{0:T(1024)} %param.20) | copy-start | bytes 122884
  1.6 7.3 %copy-start.5 = (f32[10240]{0:T(1024)S(1)}, f32[10240]{0:T(1024)}, u32[]{:S(2)}) copy-start(f32[10240]{0:T(1024)} %param.21) | copy-start | bytes 122884
  1.6 14.9 %all-to-all-start = ((bf16[32,2,640]{2,1,0:T(2,128)(2,1)}), bf16[32,2,640]{2,1,0:T(2,128)(2,1)S(1)}, u32[]{:S(2)}, u32[]{:S(2)}) async-start(bf16[32,2,640]{2,1,0:T(2,128)(2,1)} %shard_map.110), calls=%async_computation | async-start | bytes 163840 | tf_op jit(solution)/shard_map/all_to_all | solution.py:342
  8.9 7.6 %copy-start = (f32[2,4096]{1,0:T(2,128)S(1)}, f32[2,4096]{1,0:T(2,128)}, u32[]{:S(2)}) copy-start(f32[2,4096]{1,0:T(2,128)} %refs_1_.2) | copy-start | bytes 98308

commit v6 on v5

--- a/solution.py
+++ b/solution.py
@@ -16,7 +16,7 @@
 CODES = 1 << 17
 SLANT = 13
 HOLE = 1 << 24
-COMPACT_ROWS = 16
+COMPACT_ROWS = 10
 
 COEFFS = ((1.0, 1.1, 1.0, 6.0, 0.004, 0.6), (0.3, 1.4, 0.9, 8.0, 0.002, 0.7))
 LOW_LEVEL = -6.0

time: 28.5 us -> 28.5 us (level)
  no operation moved by 1% of the time
where the time goes in v6:
time: 28.5 us; the launch traced here: 28.2 us
  blocking collectives  8.95 us (31%)
  starting transfers between devices  7.3 us (26%)
  Pallas kernels  6.95 us (24%)
  waiting for transfers between devices  4.16 us (15%)
  between operations  0.75 us (3%)
    all_to_all x1, blocking collectives, exchange(): return lax.all_to_all(array, AXES, split_axis=0, concat_axis=0, tiled=True)  8.95 us
    all_to_all x1, starting transfers between devices, exchange(): return lax.all_to_all(array, AXES, split_axis=0, concat_axis=0, tiled=True)  7.3 us
    all_to_all x1, waiting for transfers between devices, exchange(): return lax.all_to_all(array, AXES, split_axis=0, concat_axis=0, tiled=True)  4.16 us
    pallas_call x1, Pallas kernels, shards(): pl.pallas_call(lambda *refs: exposure_kernel(t_dev, COMPACT_ROWS, *refs),...  3.39 us
    pallas_call x1, Pallas kernels, shards(): pl.pallas_call(lambda *refs: loss_kernel(n_ev, n_site, n_rup, *refs), out...  2.09 us
    pallas_call x1, Pallas kernels, shards(): pl.pallas_call(lambda *refs: pack_kernel(n_ev, n_site, *refs), out_shape=...  0.79 us
    pallas_call x1, Pallas kernels, shards(): pl.pallas_call(lambda *refs: total_kernel(n_ev, n_site, *refs), out_shape...  0.68 us
  transfers between devices with their start and end apart: 1, of which 1 were waited for; matrix products, arithmetic and copies ran while one was open for 0% of the time, Pallas kernels for 12%

profile of v6, /device:TPU:0, one launch (start us, length us, event | category | flops | bytes accessed | tf_op | source)
XLA Modules:
  0.0 28.2 jit_solution(15108301627119826668)
XLA Ops:
  0.0 0.0 copy-start.1
  0.0 0.0 copy-start.6
  0.7 0.0 copy-done.6
  0.7 0.1 copy.12.refs_1_
  0.8 0.0 copy-done.1
  0.8 0.8 %shard_map.110 = bf16[32,2,640]{2,1,0:T(2,128)(2,1)} custom-call(s32[8,128]{1,0:T(8,128)S(1)} %shard_map.109.refs_0_, f32[6,2]{1,0:T(8,128)S(1)} %copy.12.refs_1_, s32[1]{0:T(128)S(6)} %copy.13.refs_2_, bf16[2,4096]{1,0:T(2,128)(2,1)S(1)} %bitcast.13), custom_call_target="tpu_custom_call" | custom-call | tf_op jit(solution)/shard_map/pallas_call | solution.py:351
  1.6 0.0 copy-start.2
  1.6 0.0 copy-start.3
  1.6 0.0 copy-start.4
  1.6 0.0 copy-start.5
  1.6 7.3 %all-to-all-start = ((bf16[32,2,640]{2,1,0:T(2,128)(2,1)}), bf16[32,2,640]{2,1,0:T(2,128)(2,1)S(1)}, u32[]{:S(2)}, u32[]{:S(2)}) async-start(bf16[32,2,640]{2,1,0:T(2,128)(2,1)} %shard_map.110), calls=%async_computation | async-start | bytes 163840 | tf_op jit(solution)/shard_map/all_to_all | solution.py:342
  8.9 0.0 copy-done.2
  8.9 0.0 copy-done.3
  8.9 0.0 copy-done.4
  8.9 0.0 copy-done.5
  8.9 0.0 copy-start
  9.0 3.4 %shard_map.111 = (bf16[512,256]{1,0:T(8,128)(2,1)S(1)}, bf16[32,128]{1,0:T(8,128)(2,1)S(1)}) custom-call(s32[80,128]{1,0:T(8,128)S(1)} %bitcast.14, s32[80,128]{1,0:T(8,128)S(1)} %bitcast.15, s32[80,128]{1,0:T(8,128)S(1)} %bitcast.16, f32[80,128]{1,0:T(8,128)S(1)} %bitcast.17, bf16[40,128]{1,0:T(8,128)(2,1)} %bitcast.18, s32[1,128]{1,0:T(1,128)} %bitcast.19, ...), custom_call_target="tpu_custom_call" | custom-call | flops 2684354560 | bytes 1048576 | tf_op jit(solution)/shard_map/pallas_call | solution.py:363
  12.4 4.2 %all-to-all-done.refs_0_ = bf16[32,2,640]{2,1,0:T(2,128)(2,1)S(1)} async-done(((bf16[32,2,640]{2,1,0:T(2,128)(2,1)}), bf16[32,2,640]{2,1,0:T(2,128)(2,1)S(1)}, u32[]{:S(2)}, u32[]{:S(2)}) %all-to-all-start) | async-done | bytes 81952 | tf_op jit(solution)/shard_map/all_to_all | solution.py:342
  16.5 0.0 copy-done
  16.5 2.1 %shard_map.112 = f32[64,128]{1,0:T(8,128)S(1)} custom-call(bf16[32,2,640]{2,1,0:T(2,128)(2,1)S(1)} %all-to-all-done.refs_0_, f32[2,4096]{1,0:T(2,128)S(1)} %copy-done, bf16[512,256]{1,0:T(8,128)(2,1)S(1)} %get-tuple-element.7.refs_2_, bf16[32,128]{1,0:T(8,128)(2,1)S(1)} %get-tuple-element.8.refs_3_), custom_call_target="tpu_custom_call" | custom-call | tf_op jit(solution)/shard_map/pallas_call | solution.py:389
  18.6 8.9 %all_to_all.16 = f32[32,2,128]{2,1,0:T(2,128)S(1)} all-to-all(f32[32,2,128]{2,1,0:T(2,128)S(1)} %bitcast.11), channel_id=1, replica_groups=mesh['ev'=4,'site'=8] {'ev','site'}, dimensions={0} | all-to-all | bytes 65536 | tf_op jit(solution)/shard_map/all_to_all | solution.py:342
  27.6 0.7 %shard_map.113 = f32[8,128]{1,0:T(8,128)} custom-call(f32[64,128]{1,0:T(8,128)S(1)} %bitcast.12), custom_call_target="tpu_custom_call" | custom-call | tf_op jit(solution)/shard_map/pallas_call | solution.py:402
  (1 shorter events, 0.0 us)
Async XLA Ops:
  0.0 0.8 %copy-start.1 = (bf16[2,1,4096]{2,0,1:T(2,128)(2,1)S(1)}, bf16[2,1,4096]{2,0,1:T(2,128)(2,1)}, u32[]{:S(2)}) copy-start(bf16[2,1,4096]{2,0,1:T(2,128)(2,1)} %param.13) | copy-start | bytes 49156
  0.0 0.7 %copy-start.6 = (f32[6,2]{0,1:T(2,128)S(1)}, f32[6,2]{0,1:T(2,128)}, u32[]{:S(2)}) copy-start(f32[6,2]{0,1:T(2,128)} %param.11) | copy-start | bytes 148
  1.6 7.3 %copy-start.2 = (s32[10240]{0:T(1024)S(1)}, s32[10240]{0:T(1024)}, u32[]{:S(2)}) copy-start(s32[10240]{0:T(1024)} %param.18) | copy-start | bytes 122884
  1.6 7.3 %copy-start.3 = (s32[10240]{0:T(1024)S(1)}, s32[10240]{0:T(1024)}, u32[]{:S(2)}) copy-start(s32[10240]{0:T(1024)} %param.19) | copy-start | bytes 122884
  1.6 7.3 %copy-start.4 = (s32[10240]{0:T(1024)S(1)}, s32[10240]{0:T(1024)}, u32[]{:S(2)}) copy-start(s32[10240]{0:T(1024)} %param.20) | copy-start | bytes 122884
  1.6 7.3 %copy-start.5 = (f32[10240]{0:T(1024)S(1)}, f32[10240]{0:T(1024)}, u32[]{:S(2)}) copy-start(f32[10240]{0:T(1024)} %param.21) | copy-start | bytes 122884
  1.6 14.9 %all-to-all-start = ((bf16[32,2,640]{2,1,0:T(2,128)(2,1)}), bf16[32,2,640]{2,1,0:T(2,128)(2,1)S(1)}, u32[]{:S(2)}, u32[]{:S(2)}) async-start(bf16[32,2,640]{2,1,0:T(2,128)(2,1)} %shard_map.110), calls=%async_computation | async-start | bytes 163840 | tf_op jit(solution)/shard_map/all_to_all | solution.py:342
  8.9 7.6 %copy-start = (f32[2,4096]{1,0:T(2,128)S(1)}, f32[2,4096]{1,0:T(2,128)}, u32[]{:S(2)}) copy-start(f32[2,4096]{1,0:T(2,128)} %refs_1_.2) | copy-start | bytes 98308

commit v7 on v6

--- a/solution.py
+++ b/solution.py
@@ -64,8 +64,8 @@
 
     def fill(i, carry):
         for j in range(n_site):
-            out_ref[i * n_site + j, :, :SITE_DEV] = eps[:, j * SITE_DEV : (j + 1) * SITE_DEV]
-            out_ref[i * n_site + j, :, SITE_DEV:] = row
+            own = eps[:, j * SITE_DEV : (j + 1) * SITE_DEV]
+            out_ref[i * n_site + j] = jnp.concatenate([own, row], axis=1)
         return carry
 
     lax.fori_loop(0, n_ev, fill, 0, unroll=n_ev <= 4)
@@ -255,12 +255,12 @@
             )
             position = jnp.clip((field - LOW_LEVEL) / LEVEL_STEP, 0.0, G - 1.0)
             floor = jnp.floor(position)
-            below.append(floor)
-            weight_0.append(1.0 - (position - floor))
-            weight_1.append(jnp.maximum(0.0, 1.0 - ((floor + 1.0) - position)))
+            below.append(floor.astype(BF16))
+            weight_0.append((1.0 - (position - floor)).astype(BF16))
+            weight_1.append(jnp.maximum(0.0, 1.0 - ((floor + 1.0) - position)).astype(BF16))
 
         def wide(array, e):
-            return jnp.broadcast_to(array[e : e + 1].astype(BF16), (G, SITE_DEV))
+            return jnp.broadcast_to(array[e : e + 1], (G, SITE_DEV))
 
         ratios = []
         for e in range(EVENT_BLOCK):
@@ -304,13 +304,23 @@
 
 
 def total_kernel(n_ev, n_site, got_ref, out_ref):
-    high = got_ref.shape[0] // (n_ev * n_site)
-    rows = []
+    each = got_ref.shape[0] // n_ev
+    high = each // n_site
+    row_group = lax.broadcasted_iota(jnp.int32, (ROWS, LANES), 0) // high
+    blocks = []
     for i in range(n_ev):
-        for h in range(high):
-            part = got_ref[pl.ds(i * n_site * high + h, n_site, stride=high), :]
-            rows.append(jnp.sum(part, axis=0, keepdims=True))
-    out_ref[...] = swap_groups(jnp.concatenate(rows, axis=0), n_ev, LANES // n_ev)
+        part = got_ref[i * each : i * each + ROWS, :]
+        for q in range(ROWS, each, ROWS):
+            part = part + got_ref[i * each + q : i * each + q + ROWS, :]
+        move = ROWS // 2
+        while move >= high:
+            part = part + pltpu.roll(part, move, 0)
+            move //= 2
+        if i % (ROWS // high) == 0:
+            blocks.append(part)
+        else:
+            blocks[-1] = jnp.where(row_group == i % (ROWS // high), part, blocks[-1])
+    out_ref[...] = swap_groups(jnp.concatenate(blocks, axis=0), n_ev, LANES // n_ev)
 
 
 def shards(

time: 28.5 us -> 28.4 us (level)
  no operation moved by 1% of the time
where the time goes in v7:
time: 28.4 us; the launch traced here: 28.2 us
  blocking collectives  8.95 us (32%)
  starting transfers between devices  7.3 us (26%)
  Pallas kernels  6.9 us (24%)
  waiting for transfers between devices  4.15 us (15%)
  between operations  0.75 us (3%)
    all_to_all x1, blocking collectives, exchange(): return lax.all_to_all(array, AXES, split_axis=0, concat_axis=0, tiled=True)  8.95 us
    all_to_all x1, starting transfers between devices, exchange(): return lax.all_to_all(array, AXES, split_axis=0, concat_axis=0, tiled=True)  7.3 us
    all_to_all x1, waiting for transfers between devices, exchange(): return lax.all_to_all(array, AXES, split_axis=0, concat_axis=0, tiled=True)  4.15 us
    pallas_call x1, Pallas kernels, shards(): pl.pallas_call(lambda *refs: exposure_kernel(t_dev, COMPACT_ROWS, *refs),...  3.39 us
    pallas_call x1, Pallas kernels, shards(): pl.pallas_call(lambda *refs: loss_kernel(n_ev, n_site, n_rup, *refs), out...  2.03 us
    pallas_call x1, Pallas kernels, shards(): pl.pallas_call(lambda *refs: pack_kernel(n_ev, n_site, *refs), out_shape=...  0.8 us
    pallas_call x1, Pallas kernels, shards(): pl.pallas_call(lambda *refs: total_kernel(n_ev, n_site, *refs), out_shape...  0.67 us
  transfers between devices with their start and end apart: 1, of which 1 were waited for; matrix products, arithmetic and copies ran while one was open for 0% of the time, Pallas kernels for 12%

profile of v7, /device:TPU:0, one launch (start us, length us, event | category | flops | bytes accessed | tf_op | source)
XLA Modules:
  0.0 28.2 jit_solution(15437533290105138888)
XLA Ops:
  0.0 0.0 copy-start.1
  0.0 0.0 copy-start.6
  0.7 0.0 copy-done.6
  0.7 0.1 copy.12.refs_1_
  0.8 0.0 copy-done.1
  0.8 0.8 %shard_map.110 = bf16[32,2,640]{2,1,0:T(2,128)(2,1)} custom-call(s32[8,128]{1,0:T(8,128)S(1)} %shard_map.109.refs_0_, f32[6,2]{1,0:T(8,128)S(1)} %copy.12.refs_1_, s32[1]{0:T(128)S(6)} %copy.13.refs_2_, bf16[2,4096]{1,0:T(2,128)(2,1)S(1)} %bitcast.13), custom_call_target="tpu_custom_call" | custom-call | tf_op jit(solution)/shard_map/pallas_call | solution.py:361
  1.6 0.0 copy-start.2
  1.6 0.0 copy-start.3
  1.6 0.0 copy-start.4
  1.6 0.0 copy-start.5
  1.6 7.3 %all-to-all-start = ((bf16[32,2,640]{2,1,0:T(2,128)(2,1)}), bf16[32,2,640]{2,1,0:T(2,128)(2,1)S(1)}, u32[]{:S(2)}, u32[]{:S(2)}) async-start(bf16[32,2,640]{2,1,0:T(2,128)(2,1)} %shard_map.110), calls=%async_computation | async-start | bytes 163840 | tf_op jit(solution)/shard_map/all_to_all | solution.py:352
  8.9 0.0 copy-done.2
  8.9 0.0 copy-done.3
  8.9 0.0 copy-done.4
  8.9 0.0 copy-done.5
  8.9 0.0 copy-start
  9.0 3.4 %shard_map.111 = (bf16[512,256]{1,0:T(8,128)(2,1)S(1)}, bf16[32,128]{1,0:T(8,128)(2,1)S(1)}) custom-call(s32[80,128]{1,0:T(8,128)S(1)} %bitcast.14, s32[80,128]{1,0:T(8,128)S(1)} %bitcast.15, s32[80,128]{1,0:T(8,128)S(1)} %bitcast.16, f32[80,128]{1,0:T(8,128)S(1)} %bitcast.17, bf16[40,128]{1,0:T(8,128)(2,1)} %bitcast.18, s32[1,128]{1,0:T(1,128)} %bitcast.19, ...), custom_call_target="tpu_custom_call" | custom-call | flops 2684354560 | bytes 1048576 | tf_op jit(solution)/shard_map/pallas_call | solution.py:373
  12.4 4.2 %all-to-all-done.refs_0_ = bf16[32,2,640]{2,1,0:T(2,128)(2,1)S(1)} async-done(((bf16[32,2,640]{2,1,0:T(2,128)(2,1)}), bf16[32,2,640]{2,1,0:T(2,128)(2,1)S(1)}, u32[]{:S(2)}, u32[]{:S(2)}) %all-to-all-start) | async-done | bytes 81952 | tf_op jit(solution)/shard_map/all_to_all | solution.py:352
  16.5 0.0 copy-done
  16.5 2.0 %shard_map.112 = f32[64,128]{1,0:T(8,128)S(1)} custom-call(bf16[32,2,640]{2,1,0:T(2,128)(2,1)S(1)} %all-to-all-done.refs_0_, f32[2,4096]{1,0:T(2,128)S(1)} %copy-done, bf16[512,256]{1,0:T(8,128)(2,1)S(1)} %get-tuple-element.7.refs_2_, bf16[32,128]{1,0:T(8,128)(2,1)S(1)} %get-tuple-element.8.refs_3_), custom_call_target="tpu_custom_call" | custom-call | tf_op jit(solution)/shard_map/pallas_call | solution.py:399
  18.6 8.9 %all_to_all.16 = f32[32,2,128]{2,1,0:T(2,128)S(1)} all-to-all(f32[32,2,128]{2,1,0:T(2,128)S(1)} %bitcast.11), channel_id=1, replica_groups=mesh['ev'=4,'site'=8] {'ev','site'}, dimensions={0} | all-to-all | bytes 65536 | tf_op jit(solution)/shard_map/all_to_all | solution.py:352
  27.5 0.7 %shard_map.113 = f32[8,128]{1,0:T(8,128)} custom-call(f32[64,128]{1,0:T(8,128)S(1)} %bitcast.12), custom_call_target="tpu_custom_call" | custom-call | tf_op jit(solution)/shard_map/pallas_call | solution.py:412
  (1 shorter events, 0.0 us)
Async XLA Ops:
  0.0 0.8 %copy-start.1 = (bf16[2,1,4096]{2,0,1:T(2,128)(2,1)S(1)}, bf16[2,1,4096]{2,0,1:T(2,128)(2,1)}, u32[]{:S(2)}) copy-start(bf16[2,1,4096]{2,0,1:T(2,128)(2,1)} %param.13) | copy-start | bytes 49156
  0.0 0.7 %copy-start.6 = (f32[6,2]{0,1:T(2,128)S(1)}, f32[6,2]{0,1:T(2,128)}, u32[]{:S(2)}) copy-start(f32[6,2]{0,1:T(2,128)} %param.11) | copy-start | bytes 148
  1.6 7.3 %copy-start.2 = (s32[10240]{0:T(1024)S(1)}, s32[10240]{0:T(1024)}, u32[]{:S(2)}) copy-start(s32[10240]{0:T(1024)} %param.18) | copy-start | bytes 122884
  1.6 7.3 %copy-start.3 = (s32[10240]{0:T(1024)S(1)}, s32[10240]{0:T(1024)}, u32[]{:S(2)}) copy-start(s32[10240]{0:T(1024)} %param.19) | copy-start | bytes 122884
  1.6 7.3 %copy-start.4 = (s32[10240]{0:T(1024)S(1)}, s32[10240]{0:T(1024)}, u32[]{:S(2)}) copy-start(s32[10240]{0:T(1024)} %param.20) | copy-start | bytes 122884
  1.6 7.3 %copy-start.5 = (f32[10240]{0:T(1024)S(1)}, f32[10240]{0:T(1024)}, u32[]{:S(2)}) copy-start(f32[10240]{0:T(1024)} %param.21) | copy-start | bytes 122884
  1.6 14.9 %all-to-all-start = ((bf16[32,2,640]{2,1,0:T(2,128)(2,1)}), bf16[32,2,640]{2,1,0:T(2,128)(2,1)S(1)}, u32[]{:S(2)}, u32[]{:S(2)}) async-start(bf16[32,2,640]{2,1,0:T(2,128)(2,1)} %shard_map.110), calls=%async_computation | async-start | bytes 163840 | tf_op jit(solution)/shard_map/all_to_all | solution.py:352
  8.9 7.6 %copy-start = (f32[2,4096]{1,0:T(2,128)S(1)}, f32[2,4096]{1,0:T(2,128)}, u32[]{:S(2)}) copy-start(f32[2,4096]{1,0:T(2,128)} %refs_1_.2) | copy-start | bytes 98308

commit v8 on v7

--- a/solution.py
+++ b/solution.py
@@ -215,9 +215,9 @@
     zero = jnp.zeros((G, SITE_DEV), BF16)
     curve = curve_ref[...]
     exposure = exp_ref[...]
-    diagonal = lax.broadcasted_iota(jnp.int32, (t_dev, n_col), 0) == (
-        lax.broadcasted_iota(jnp.int32, (t_dev, n_col), 1) % t_dev
-    )
+    own_taxo = lax.broadcasted_iota(jnp.int32, (ROWS, n_col), 1) % t_dev
+    diagonal = lax.broadcasted_iota(jnp.int32, (ROWS, n_col), 0) == own_taxo % ROWS
+    taxo_rows = own_taxo // ROWS
 
     def joined(array):
         return (array + pltpu.roll(array, LANES - PART, 1)) + pltpu.roll(array, LANES - 2 * PART, 1)
@@ -280,10 +280,12 @@
                 ratio_s[(e + 1) * t_dev - 32 : (e + 1) * t_dev, :] = jnp.concatenate(ratios, axis=0)
                 ratios = []
         terms = jnp.dot(ratio_s[...], exposure, preferred_element_type=F32)
-        rows = [
-            jnp.sum(jnp.where(diagonal, terms[e * t_dev : (e + 1) * t_dev], 0.0), axis=0, keepdims=True)
-            for e in range(EVENT_BLOCK)
-        ]
+        rows = []
+        for e in range(EVENT_BLOCK):
+            part = terms[e * t_dev : e * t_dev + ROWS]
+            for q in range(1, t_dev // ROWS):
+                part = jnp.where(taxo_rows == q, terms[e * t_dev + q * ROWS : e * t_dev + (q + 1) * ROWS], part)
+            rows.append(jnp.sum(jnp.where(diagonal, part, 0.0), axis=0, keepdims=True))
         loss_s[pl.ds(first, EVENT_BLOCK), :] = jnp.concatenate(rows, axis=0)
         return carry
 

time: 28.4 us -> 28.4 us (level)
  no operation moved by 1% of the time
where the time goes in v8:
time: 28.4 us; the launch traced here: 28.2 us
  blocking collectives  8.95 us (32%)
  starting transfers between devices  7.3 us (26%)
  Pallas kernels  6.87 us (24%)
  waiting for transfers between devices  4.15 us (15%)
  between operations  0.75 us (3%)
    all_to_all x1, blocking collectives, exchange(): return lax.all_to_all(array, AXES, split_axis=0, concat_axis=0, tiled=True)  8.95 us
    all_to_all x1, starting transfers between devices, exchange(): return lax.all_to_all(array, AXES, split_axis=0, concat_axis=0, tiled=True)  7.3 us
    all_to_all x1, waiting for transfers between devices, exchange(): return lax.all_to_all(array, AXES, split_axis=0, concat_axis=0, tiled=True)  4.15 us
    pallas_call x1, Pallas kernels, shards(): pl.pallas_call(lambda *refs: exposure_kernel(t_dev, COMPACT_ROWS, *refs),...  3.39 us
    pallas_call x1, Pallas kernels, shards(): pl.pallas_call(lambda *refs: loss_kernel(n_ev, n_site, n_rup, *refs), out...  2.01 us
    pallas_call x1, Pallas kernels, shards(): pl.pallas_call(lambda *refs: pack_kernel(n_ev, n_site, *refs), out_shape=...  0.8 us
    pallas_call x1, Pallas kernels, shards(): pl.pallas_call(lambda *refs: total_kernel(n_ev, n_site, *refs), out_shape...  0.67 us
  transfers between devices with their start and end apart: 1, of which 1 were waited for; matrix products, arithmetic and copies ran while one was open for 0% of the time, Pallas kernels for 12%

profile of v8, /device:TPU:0, one launch (start us, length us, event | category | flops | bytes accessed | tf_op | source)
XLA Modules:
  0.0 28.2 jit_solution(6812886263058042272)
XLA Ops:
  0.0 0.0 copy-start.1
  0.0 0.0 copy-start.6
  0.7 0.0 copy-done.6
  0.7 0.1 copy.12.refs_1_
  0.8 0.0 copy-done.1
  0.8 0.8 %shard_map.110 = bf16[32,2,640]{2,1,0:T(2,128)(2,1)} custom-call(s32[8,128]{1,0:T(8,128)S(1)} %shard_map.109.refs_0_, f32[6,2]{1,0:T(8,128)S(1)} %copy.12.refs_1_, s32[1]{0:T(128)S(6)} %copy.13.refs_2_, bf16[2,4096]{1,0:T(2,128)(2,1)S(1)} %bitcast.13), custom_call_target="tpu_custom_call" | custom-call | tf_op jit(solution)/shard_map/pallas_call | solution.py:363
  1.6 0.0 copy-start.2
  1.6 0.0 copy-start.3
  1.6 0.0 copy-start.4
  1.6 0.0 copy-start.5
  1.6 7.3 %all-to-all-start = ((bf16[32,2,640]{2,1,0:T(2,128)(2,1)}), bf16[32,2,640]{2,1,0:T(2,128)(2,1)S(1)}, u32[]{:S(2)}, u32[]{:S(2)}) async-start(bf16[32,2,640]{2,1,0:T(2,128)(2,1)} %shard_map.110), calls=%async_computation | async-start | bytes 163840 | tf_op jit(solution)/shard_map/all_to_all | solution.py:354
  8.9 0.0 copy-done.2
  8.9 0.0 copy-done.3
  8.9 0.0 copy-done.4
  8.9 0.0 copy-done.5
  8.9 0.0 copy-start
  9.0 3.4 %shard_map.111 = (bf16[512,256]{1,0:T(8,128)(2,1)S(1)}, bf16[32,128]{1,0:T(8,128)(2,1)S(1)}) custom-call(s32[80,128]{1,0:T(8,128)S(1)} %bitcast.14, s32[80,128]{1,0:T(8,128)S(1)} %bitcast.15, s32[80,128]{1,0:T(8,128)S(1)} %bitcast.16, f32[80,128]{1,0:T(8,128)S(1)} %bitcast.17, bf16[40,128]{1,0:T(8,128)(2,1)} %bitcast.18, s32[1,128]{1,0:T(1,128)} %bitcast.19, ...), custom_call_target="tpu_custom_call" | custom-call | flops 2684354560 | bytes 1048576 | tf_op jit(solution)/shard_map/pallas_call | solution.py:375
  12.4 4.2 %all-to-all-done.refs_0_ = bf16[32,2,640]{2,1,0:T(2,128)(2,1)S(1)} async-done(((bf16[32,2,640]{2,1,0:T(2,128)(2,1)}), bf16[32,2,640]{2,1,0:T(2,128)(2,1)S(1)}, u32[]{:S(2)}, u32[]{:S(2)}) %all-to-all-start) | async-done | bytes 81952 | tf_op jit(solution)/shard_map/all_to_all | solution.py:354
  16.5 0.0 copy-done
  16.5 2.0 %shard_map.112 = f32[64,128]{1,0:T(8,128)S(1)} custom-call(bf16[32,2,640]{2,1,0:T(2,128)(2,1)S(1)} %all-to-all-done.refs_0_, f32[2,4096]{1,0:T(2,128)S(1)} %copy-done, bf16[512,256]{1,0:T(8,128)(2,1)S(1)} %get-tuple-element.7.refs_2_, bf16[32,128]{1,0:T(8,128)(2,1)S(1)} %get-tuple-element.8.refs_3_), custom_call_target="tpu_custom_call" | custom-call | tf_op jit(solution)/shard_map/pallas_call | solution.py:401
  18.5 8.9 %all_to_all.16 = f32[32,2,128]{2,1,0:T(2,128)S(1)} all-to-all(f32[32,2,128]{2,1,0:T(2,128)S(1)} %bitcast.11), channel_id=1, replica_groups=mesh['ev'=4,'site'=8] {'ev','site'}, dimensions={0} | all-to-all | bytes 65536 | tf_op jit(solution)/shard_map/all_to_all | solution.py:354
  27.5 0.7 %shard_map.113 = f32[8,128]{1,0:T(8,128)} custom-call(f32[64,128]{1,0:T(8,128)S(1)} %bitcast.12), custom_call_target="tpu_custom_call" | custom-call | tf_op jit(solution)/shard_map/pallas_call | solution.py:414
  (1 shorter events, 0.0 us)
Async XLA Ops:
  0.0 0.8 %copy-start.1 = (bf16[2,1,4096]{2,0,1:T(2,128)(2,1)S(1)}, bf16[2,1,4096]{2,0,1:T(2,128)(2,1)}, u32[]{:S(2)}) copy-start(bf16[2,1,4096]{2,0,1:T(2,128)(2,1)} %param.13) | copy-start | bytes 49156
  0.0 0.7 %copy-start.6 = (f32[6,2]{0,1:T(2,128)S(1)}, f32[6,2]{0,1:T(2,128)}, u32[]{:S(2)}) copy-start(f32[6,2]{0,1:T(2,128)} %param.11) | copy-start | bytes 148
  1.6 7.3 %copy-start.2 = (s32[10240]{0:T(1024)S(1)}, s32[10240]{0:T(1024)}, u32[]{:S(2)}) copy-start(s32[10240]{0:T(1024)} %param.18) | copy-start | bytes 122884
  1.6 7.3 %copy-start.3 = (s32[10240]{0:T(1024)S(1)}, s32[10240]{0:T(1024)}, u32[]{:S(2)}) copy-start(s32[10240]{0:T(1024)} %param.19) | copy-start | bytes 122884
  1.6 7.3 %copy-start.4 = (s32[10240]{0:T(1024)S(1)}, s32[10240]{0:T(1024)}, u32[]{:S(2)}) copy-start(s32[10240]{0:T(1024)} %param.20) | copy-start | bytes 122884
  1.6 7.3 %copy-start.5 = (f32[10240]{0:T(1024)S(1)}, f32[10240]{0:T(1024)}, u32[]{:S(2)}) copy-start(f32[10240]{0:T(1024)} %param.21) | copy-start | bytes 122884
  1.6 14.9 %all-to-all-start = ((bf16[32,2,640]{2,1,0:T(2,128)(2,1)}), bf16[32,2,640]{2,1,0:T(2,128)(2,1)S(1)}, u32[]{:S(2)}, u32[]{:S(2)}) async-start(bf16[32,2,640]{2,1,0:T(2,128)(2,1)} %shard_map.110), calls=%async_computation | async-start | bytes 163840 | tf_op jit(solution)/shard_map/all_to_all | solution.py:354
  8.9 7.6 %copy-start = (f32[2,4096]{1,0:T(2,128)S(1)}, f32[2,4096]{1,0:T(2,128)}, u32[]{:S(2)}) copy-start(f32[2,4096]{1,0:T(2,128)} %refs_1_.2) | copy-start | bytes 98308
